TPU v7x, 512 devices: a whole 4x8x8 slice. The times are simulated.
512 devices in a mesh: narrow: 8 (over y), ep: 64 (over z, x, core).
Axes of the slice: x: 4, y: 8, z: 8, core: 2. Of those that a mesh axis runs over, the one named last changes fastest.
Arguments:
- queries: bfloat16 [2048, 128, 576], P('ep', 'narrow'), may hold values from -6 to 6
- trunk_cache: bfloat16 [128, 768, 576], P('ep'), may hold values from -6 to 6
- branch_cache: bfloat16 [128, 16, 32, 576], P('ep'), may hold values from -6 to 6
- visible: int32 [128, 16, 16], P('ep'), may hold values from 0 to 1, as said below
- branch_len: int32 [128, 16], P('ep'), may hold values from 1 to 32, as said below
- value_up: bfloat16 [128, 512, 128], P('narrow'), may hold values from -0.25 to 0.25
- out_proj: bfloat16 [16384, 7168], P('narrow', 'ep'), may hold values from -0.1875 to 0.1875
- residual_in: bfloat16 [2048, 7168], P('narrow', 'ep'), may hold values from -4 to 4
- norm_gain: float32 [7168], replicated, may hold values from 0.25 to 1.75
- expert_ids: int32 [2048, 8], P('narrow'), may hold values from 0 to 255, all different within a row; in each aligned block of 256 rows (0 to 255, 256 to 511, ...) at most 16 rows name the same one
Outputs:
- hidden: bfloat16 [2048, 7168], P('narrow', 'ep')
- expert_inputs: bfloat16 [8, 256, 16, 7168], P('narrow', 'ep')
Inputs may be any that keep to these rules, and one draw needn't show every extreme that they name: visible[r, b, b] = 1, branch 0 is the root of its tree, and the ones of a row are b and its chain of ancestors. `branch_len`: every tree has a branch of exactly 32 positions. `expert_ids`: within one block of 256 tokens no expert is chosen more than 16 times.
All inputs are finite; a program needn't handle non-finite values.
Results may differ from a plain program's by a relative error of at most 0.0066.
Values may be sent and summed in bfloat16 or wider, within the bound.
A program may use at most 64 MiB of HBM per device.

v0:
```python
import jax
import jax.numpy as jnp
from jax import lax
from jax.sharding import PartitionSpec as P

LAT = 512
EXP_DEV = 4


score_scale = 192.0 ** (-0.5)
norm_eps = 1e-06


def tree_attention(query, trunk, branch, visible, length):
    branches, slots, kdim = branch.shape
    keys = branch.reshape(branches * slots, kdim)
    trunk_scores = (
        jnp.einsum("bhk,pk->bhp", query, trunk, preferred_element_type=jnp.float32) * score_scale
    )
    branch_scores = (
        jnp.einsum("bhk,pk->bhp", query, keys, preferred_element_type=jnp.float32) * score_scale
    )
    position = jnp.arange(slots, dtype=jnp.int32)
    live = (visible[:, :, None] > 0) & (position[None, None, :] < length[None, :, None])
    live = live.reshape(branches, 1, branches * slots)
    branch_scores = jnp.where(live, branch_scores, -jnp.inf)
    scores = jnp.concatenate([trunk_scores, branch_scores], axis=-1)
    top_score = jnp.max(scores, axis=-1, keepdims=True)
    expo = jnp.exp(scores - top_score)
    weights = (expo / jnp.sum(expo, axis=-1, keepdims=True)).astype(jnp.bfloat16)
    values = jnp.concatenate([trunk[:, :LAT], keys[:, :LAT]], axis=0)
    latent_out = jnp.einsum("bhp,pl->bhl", weights, values, preferred_element_type=jnp.float32)
    return latent_out.astype(jnp.bfloat16)


def shards(
    queries,
    trunk_cache,
    branch_cache,
    visible,
    branch_len,
    value_up,
    out_proj,
    residual_in,
    norm_gain,
    expert_ids,
):
    trees_here, branches = branch_len.shape
    heads_here = value_up.shape[0]
    grouped = queries.reshape(trees_here, branches, heads_here, queries.shape[2])

    def per_tree(items):
        latent_out = tree_attention(*items)
        feats = jnp.einsum("bhl,hlv->bhv", latent_out, value_up, preferred_element_type=jnp.float32)
        return feats.astype(jnp.bfloat16).reshape(branches, heads_here * value_up.shape[2])

    features = lax.map(per_tree, (grouped, trunk_cache, branch_cache, visible, branch_len))
    features = features.reshape(trees_here * branches, heads_here * value_up.shape[2])
    partial_rows = jnp.dot(
        lax.all_gather(features, "ep", axis=0, tiled=True),
        out_proj,
        preferred_element_type=jnp.float32,
    )
    projected = lax.psum_scatter(partial_rows, "narrow", scatter_dimension=0, tiled=True)
    hidden = (residual_in.astype(jnp.float32) + projected).astype(jnp.bfloat16)
    hidden_f = hidden.astype(jnp.float32)
    ep_count = lax.axis_size("ep")
    columns = hidden.shape[1]
    width = columns * ep_count
    block_rows, top = expert_ids.shape
    experts = EXP_DEV * ep_count
    slots = 2 * block_rows * top // experts
    local_squares = jnp.sum(hidden_f * hidden_f, axis=-1)
    total_squares = lax.psum(local_squares, "ep")
    gain_here = lax.dynamic_slice_in_dim(norm_gain, lax.axis_index("ep") * columns, columns, 0)
    scale = lax.rsqrt(total_squares / width + norm_eps)
    payload = (hidden_f * scale[:, None] * gain_here[None, :]).astype(jnp.bfloat16)
    flat_ids = expert_ids.reshape(block_rows * top)
    onehot = (flat_ids[:, None] == jnp.arange(experts, dtype=jnp.int32)[None, :]).astype(jnp.int32)
    before = jnp.cumsum(onehot, axis=0) - onehot
    slot = jnp.sum(before * onehot, axis=1)
    target = (flat_ids * slots + slot).reshape(block_rows, top)
    chosen = jnp.any(
        target[None, :, :] == jnp.arange(experts * slots, dtype=jnp.int32)[:, None, None], axis=-1
    )
    outgoing = jnp.dot(
        chosen.astype(jnp.bfloat16), payload, preferred_element_type=jnp.float32
    ).astype(jnp.bfloat16)
    outgoing = outgoing.reshape(ep_count, EXP_DEV, slots, columns)
    arrived = lax.all_to_all(outgoing, "ep", split_axis=0, concat_axis=3, tiled=True)
    return (hidden, arrived)


def solution(mesh):
    placed = (
        P("ep", "narrow", None),
        P("ep", None, None),
        P("ep", None, None, None),
        P("ep", None, None),
        P("ep", None),
        P("narrow", None, None),
        P("narrow", "ep"),
        P("narrow", "ep"),
        P(),
        P("narrow", None),
    )
    return jax.shard_map(
        shards,
        mesh=mesh,
        in_specs=placed,
        out_specs=(P("narrow", "ep"), P("narrow", "ep", None, None)),
        check_vma=False,
    )
```

profile of v0, /device:TPU:1, one launch (start us, length us, event | category | flops | bytes accessed | tf_op | source)
XLA Modules:
  0.0 342.7 jit_solution(486198861142247539)
XLA Ops:
  7.2 0.0 copy-start
  7.2 0.0 all-gather.2.cloned.1.call-start
  7.2 0.0 copy-start.7
  7.2 18.4 %while.10 = (s32[]{:T(128)}, bf16[2,16,2048]{2,1,0:T(8,128)(2,1)S(1)}, bf16[2,16,16,576]{3,2,1,0:T(8,128)(2,1)}, bf16[2,768,576]{1,2,0:T(8,128)(2,1)}, s32[2,16,...) while((s32[]{:T(128)}, ...), condition=%wide.region_4.5_spmd, body=%wide.region_0.4_spmd.sunk | while | flops 752460032 | bytes 24696260 | solution.py:57
  7.3 1.2 constant_dynamic-slice_fusion.3
  8.5 0.0 copy-start.4
  8.5 0.2 copy.76
  8.7 1.2 dynamic-slice_bitcast_fusion.2
  10.0 0.1 and.28
  10.1 0.1 and.29
  10.3 0.1 lt.38
  10.3 0.1 broadcast_reduce_fusion.2
  10.4 0.1 lt.39
  10.6 0.5 fusion.58
  11.1 1.7 fusion.59
  12.8 0.3 fusion.60
  13.1 0.3 divide_convert_fusion.2
  13.5 0.5 slice-done
  13.9 2.4 fusion.61
  16.5 1.1 constant_dynamic-slice_fusion.3
  17.7 0.0 copy-start.4
  17.7 0.0 copy-start.2
  17.7 0.2 copy.76
  17.9 1.2 dynamic-slice_bitcast_fusion.2
  19.2 0.1 and.28
  19.3 0.1 and.29
  19.4 0.1 lt.38
  19.5 0.1 broadcast_reduce_fusion.2
  19.6 0.1 lt.39
  19.7 0.5 fusion.58
  20.2 1.7 fusion.59
  22.0 0.0 slice-start
  22.0 0.3 fusion.60
  22.3 0.3 divide_convert_fusion.2
  22.7 0.5 slice-done
  23.1 2.4 fusion.61
  25.6 0.0 copy-start.3
  25.7 0.6 copy-done.3
  26.3 0.0 all-gather.2.cloned.1.call-update
  26.3 0.2 reduce-scatter.2.cloned.1.call-start
  26.6 0.1 copy.57
  26.7 0.1 eq.42
  26.8 0.1 eq.38
  26.9 0.1 copy.59
  27.0 95.1 %all-gather.2.cloned.1.call-done = bf16[2048,2048]{1,0:T(8,128)(2,1)} async-done(((bf16[32,2048]{1,0:T(8,128)(2,1)}), bf16[2048,2048]{1,0:T(8,128)(2,1)}) %all-gather.2.cloned.1.call-update) | async-done | bytes 8388624 | tf_op jit(solution)/shard_map/all_gather | solution.py:60
  122.1 7.1 %fusion.38 = f32[2048,112]{0,1:T(8,128)} fusion(bf16[2048,2048]{1,0:T(8,128)(2,1)} %all-gather.2.cloned.1.call-done, bf16[2048,112]{0,1:T(8,128)(2,1)S(1)} %copy-done), kind=kOutput, calls=%fused_computation.59 | convolution fusion | flops 939524096 | bytes 9764864 | tf_op jit(solution)/shard_map/dot_general | solution.py:59
  129.3 0.0 reduce-scatter.2.cloned.1.call-update
  129.3 0.3 fusion.27
  129.7 0.2 broadcast_add_fusion
  129.9 1.2 copy.60
  131.2 0.0 copy-start.5
  131.2 0.9 fusion.26
  132.1 0.1 reduce_sum.30
  132.2 0.1 copy.61
  132.3 0.8 dynamic_slice.25
  133.1 37.4 %fusion.24 = pred[4096,256]{1,0:T(8,128)(4,1)S(1)} fusion(s32[256,8]{0,1:T(8,128)S(1)} %multiply_add_fusion), kind=kLoop, calls=%fused_computation.35 | loop fusion | flops 15728640 | bytes 1056768 | tf_op jit(solution)/shard_map/reduce_or | solution.py:83
  170.4 0.0 reduce-scatter.2.cloned.1.call-done
  170.5 0.9 fusion.30
  171.4 123.7 %psum.7 = f32[256]{0:T(256)S(1)} all-reduce(f32[256]{0:T(256)S(1)} %get-tuple-element.69), channel_id=1, replica_groups=mesh['narrow'=8,'ep'=64] {'ep'}, use_global_device_ids=true, to_apply=%region_11.12 | all-reduce | flops 256 | bytes 2048 | tf_op jit(solution)/shard_map/psum | solution.py:74
  295.1 0.8 convolution_convert_fusion
  295.9 0.7 copy.62
  296.6 35.4 %all_to_all.18 = bf16[64,4,16,112]{3,2,1,0:T(8,128)(2,1)S(1)} all-to-all(bf16[64,4,16,112]{3,2,1,0:T(8,128)(2,1)S(1)} %bitcast.87), channel_id=1, replica_groups=mesh['narrow'=8,'ep'=64] {'ep'}, dimensions={0} | all-to-all | bytes 1835008 | tf_op jit(solution)/shard_map/all_to_all | solution.py:90
  332.0 0.7 copy.63
  332.7 3.2 all_to_all.16
  (45 shorter events, 0.4 us)
Async XLA Ops:
  7.2 115.0 %copy-start = (bf16[2048,112]{0,1:T(8,128)(2,1)S(1)}, bf16[2048,112]{0,1:T(8,128)(2,1)}, u32[]{:S(2)}) copy-start(bf16[2048,112]{0,1:T(8,128)(2,1)} %param.18) | copy-start | bytes 1376260
  7.2 115.0 %all-gather.2.cloned.1.call-start = ((), (), s32[]{:S(2)}) async-start(), calls=%async_computation.2 | async-start | bytes 8519680 | tf_op jit(solution)/shard_map/all_gather | solution.py:60
  7.2 19.3 %copy-start.7 = (s32[256,8]{0,1:T(8,128)S(1)}, s32[256,8]{0,1:T(8,128)}, u32[]{:S(2)}) copy-start(s32[256,8]{0,1:T(8,128)} %param.21) | copy-start | bytes 24580
  8.5 1.5 copy-start.4
  8.5 1.8 copy-start.8
  8.5 2.0 copy-start.2
  10.0 2.8 copy-start.1
  12.8 1.1 slice-start
  17.7 1.5 copy-start.4
  17.7 1.8 copy-start.8
  17.7 2.0 copy-start.2
  19.2 2.8 copy-start.1
  22.0 1.1 slice-start
  25.6 0.7 copy-start.3
  26.3 144.1 %reduce-scatter.2.cloned.1.call-start = ((), (), s32[]{:S(2)}) async-start(), calls=%async_computation.3 | async-start | bytes 1032192 | tf_op jit(solution)/shard_map/reduce_scatter | solution.py:64
  131.2 39.3 %copy-start.5 = (bf16[256,112]{0,1:T(8,128)(2,1)S(1)}, bf16[256,112]{0,1:T(8,128)(2,1)}, u32[]{:S(2)}) copy-start(bf16[256,112]{0,1:T(8,128)(2,1)} %param.19) | copy-start | bytes 172036
  171.4 125.2 %copy-start.6 = (bf16[256,112]{0,1:T(8,128)(2,1)}, bf16[256,112]{0,1:T(8,128)(2,1)S(1)}, u32[]{:S(2)}) copy-start(bf16[256,112]{0,1:T(8,128)(2,1)S(1)} %get-tuple-element.70) | copy-start | bytes 172036
Sparse Core Ops, SparseCore 0:
  26.4 95.6 all-gather.1
  129.4 31.4 reduce-scatter.1
where the time goes:
time: 343 us
  blocking collectives  159 us (46%)
  waiting for transfers between devices  95.2 us (28%)
  other arithmetic  41.2 us (12%)
  matrix products  17.2 us (5%)
  local copies, waits for them, and re-layouts  15.2 us (4%)
  between operations  14.2 us (4%)
    psum x1, blocking collectives, shards(): total_squares = lax.psum(local_squares, 'ep')  124 us
    all_gather x1, waiting for transfers between devices, shards(): lax.all_gather(features, 'ep', axis=0, tiled=True)  95.1 us
    reduce_or x1, other arithmetic, shards(): jnp.any(target[None, :, :] == jnp.arange(experts * slots, dtype=jnp.int32...  37.4 us
    all_to_all x1, blocking collectives, shards(): lax.all_to_all(outgoing, 'ep', split_axis=0, concat_axis=3, tiled=True)  35.4 us
    dot_general x1, matrix products, shards(): jnp.dot(lax.all_gather(features, 'ep', axis=0, tiled=True), out_proj, pre...  7.12 us
  transfers between devices with their start and end apart: 2, of which 1 were waited for; matrix products, arithmetic and copies ran while one was open for 12% of the time, Pallas kernels for 0%

commit v1 on v0

v1 whole, which is shorter than its diff:
```python
import functools

import jax
import jax.numpy as jnp
from jax import lax
from jax.experimental import pallas as pl
from jax.experimental.pallas import tpu as pltpu
from jax.sharding import PartitionSpec as P

NX = 4
GROUP = 2 * NX
EXP_DEV = 4
SLOTS = 16

score_scale = 192.0 ** (-0.5)
norm_eps = 1e-06

MESH = pl.DeviceIdType.MESH
NT = (((1,), (1,)), ((), ()))
NN = (((1,), (0,)), ((), ()))


def matmul(a, b, dims=NN):
    return lax.dot_general(a, b, dims, preferred_element_type=jnp.float32)


class Ids:
    def __init__(self):
        self.names = {}

    def __call__(self, *name):
        return self.names.setdefault(name, len(self.names))


def kernel(
    cfg,
    q_hbm,
    trunk_hbm,
    branch_hbm,
    vup_hbm,
    w_hbm,
    vis_ref,
    len_ref,
    res_ref,
    gain_ref,
    ids_ref,
    hid_ref,
    out_ref,
    q_ref,
    trunk_ref,
    branch_ref,
    vup_ref,
    s_ref,
    p_ref,
    bias_ref,
    lat_ref,
    feat_ref,
    w_ref,
    rt_ref,
    rb_ref,
    part_ref,
    part16_ref,
    got_ref,
    h_ref,
    onehot_ref,
    picked_ref,
    in_sem,
    send_sem,
    recv_sem,
):
    ny, nz, sem_count = cfg
    trees, rows, kdim = q_ref.shape
    trunk_len = trunk_ref.shape[2]
    nkeys = branch_ref.shape[1]
    heads, lat, vdim = vup_ref.shape
    branches = vis_ref.shape[1]
    brmost = nkeys // branches
    cols = w_hbm.shape[0]
    cz = GROUP * cols
    toks = trees * branches
    block = GROUP * toks
    width = nz * cz
    bf16, f32, i32 = jnp.bfloat16, jnp.float32, jnp.int32

    y = lax.axis_index("narrow")
    ep = lax.axis_index("ep")
    z = ep // GROUP
    j = ep % GROUP
    x = j // 2
    core = j % 2

    def at(dy=0, dz=0, dx=0, flip=False):
        yy = (y + dy) % ny
        zz = (z + dz) % nz
        xx = (x + dx) % NX
        cc = 1 - core if flip else core
        return (yy, zz * GROUP + xx * 2 + cc)

    barrier = pltpu.get_barrier_semaphore()
    partners = [at(dz=1), at(dz=-1)]
    partners += [(y, z * GROUP + (j + k) % GROUP) for k in range(1, GROUP)]
    partners += [at(dy=d) for d in range(1, ny)]
    for p in partners:
        pl.semaphore_signal(barrier, inc=1, device_id=p, device_id_type=MESH)

    loads = []

    def load(src, dst):
        c = pltpu.make_async_copy(src, dst, in_sem.at[len(loads)])
        c.start()
        loads.append(c)
        return c

    def w_rows(jj, lo=0, hi=None):
        hi = cols if hi is None else hi
        return w_ref.at[pl.ds(pl.multiple_of(jj * cols + lo, 16), hi - lo), :]

    tree_loads = []
    for t in range(trees):
        tree_loads.append(
            [
                load(q_hbm.at[t], q_ref.at[t]),
                load(trunk_hbm.at[t], trunk_ref.at[t]),
                load(branch_hbm.at[t], branch_ref.at[t]),
            ]
        )
    vup_load = load(vup_hbm, vup_ref)
    own_w = load(w_hbm, w_rows(j))

    res = res_ref[...]
    fill = 128 - cols
    if fill:
        res = jnp.concatenate([res, jnp.zeros((fill, block), bf16)], axis=0)
    ri = lax.broadcasted_iota(i32, (block, block), 0)
    ci = lax.broadcasted_iota(i32, (block, block), 1)
    eye = (ri == ci).astype(f32).astype(bf16)
    rt_ref[...] = matmul(eye, res, NT).astype(bf16).reshape(GROUP, toks, 128)

    sends = []
    ids = Ids()

    def copy(name, src, dst, dev):
        i = ids(*name)
        c = pltpu.make_async_remote_copy(
            src_ref=src,
            dst_ref=dst,
            send_sem=send_sem.at[i],
            recv_sem=recv_sem.at[i],
            device_id=dev,
            device_id_type=MESH,
        )
        c.start()
        sends.append(c)

    def arrived(name, dst):
        i = ids(*name)
        pltpu.make_async_remote_copy(
            src_ref=dst,
            dst_ref=dst,
            send_sem=send_sem.at[i],
            recv_sem=recv_sem.at[i],
            device_id=at(flip=True),
            device_id_type=MESH,
        ).wait_recv()

    pl.semaphore_wait(barrier, len(partners))

    wsplit = (cols // 16 + 1) // 2 * 16
    copy(("w", 1), w_hbm, w_rows(j), at(dx=1))
    copy(("w", -1), w_hbm, w_rows(j), at(dx=-1))
    copy(("ws", 0), w_hbm, w_rows(j), at(flip=True))
    for k in range(1, GROUP):
        jj = (j + k) % GROUP
        copy(("r", k), rt_ref.at[jj], rb_ref.at[j], (y, z * GROUP + jj))

    def xj(dx):
        return ((x + dx) % NX) * 2 + core

    def xj_other(dx):
        return ((x + dx) % NX) * 2 + (1 - core)

    for t in range(trees):
        for c in tree_loads[t]:
            c.wait()
        key_i = lax.broadcasted_iota(i32, (branches, nkeys), 1)
        owner = key_i // brmost
        pos = key_i % brmost
        vis = jnp.zeros((branches, nkeys), i32)
        lim = jnp.zeros((branches, nkeys), i32)
        for b in range(branches):
            here = owner == b
            vis = jnp.where(here, vis_ref[t, :, b : b + 1], vis)
            lim = jnp.where(here, len_ref[t : t + 1, b : b + 1], lim)
        live = (vis > 0) & (pos < lim)
        bias_ref[...] = jnp.where(live, 0.0, -1e30)

        q = q_ref[t]
        s_ref[:, :trunk_len] = matmul(q, trunk_ref[t])
        s_ref[:, trunk_len:] = matmul(q, branch_ref[t], NT)

        def soft(b, carry):
            r = pl.ds(pl.multiple_of(b * heads, heads), heads)
            st = s_ref[r, :trunk_len] * score_scale
            sb = s_ref[r, trunk_len:] * score_scale + bias_ref[pl.ds(b, 1), :]
            top = jnp.maximum(
                jnp.max(st, axis=-1, keepdims=True), jnp.max(sb, axis=-1, keepdims=True)
            )
            et = jnp.exp(st - top)
            eb = jnp.exp(sb - top)
            inv = 1.0 / (
                jnp.sum(et, axis=-1, keepdims=True) + jnp.sum(eb, axis=-1, keepdims=True)
            )
            p_ref[r, :trunk_len] = (et * inv).astype(bf16)
            p_ref[r, trunk_len:] = (eb * inv).astype(bf16)
            return carry

        lax.fori_loop(0, branches, soft, 0, unroll=4)
        o = matmul(p_ref[:, :trunk_len], trunk_ref[t, :lat, :], NT)
        o = o + matmul(p_ref[:, trunk_len:], branch_ref[t, :, :lat])
        o = o.astype(bf16)
        ro = lax.broadcasted_iota(i32, (rows, rows), 0)
        co = lax.broadcasted_iota(i32, (rows, rows), 1)
        swap = (co == (ro % branches) * heads + ro // branches).astype(f32).astype(bf16)
        o = matmul(swap, o).astype(bf16)
        lat_ref[:, t * branches : (t + 1) * branches, :] = o.reshape(heads, branches, lat)

    vup_load.wait()
    for h in range(heads):
        f = matmul(lat_ref[h], vup_ref[h])
        feat_ref[0, :, h * vdim : (h + 1) * vdim] = f.astype(bf16)

    half_z = nz // 2
    mid = toks // 2

    def f_part(slot, step, way):
        if step == half_z:
            return feat_ref.at[slot, (slice(0, mid) if way > 0 else slice(mid, toks)), :]
        return feat_ref.at[slot]

    def f_send(step):
        for way in (1, -1):
            src = (-way * (step - 1)) % nz
            dst = (-way * step) % nz
            copy(("f", way, step), f_part(src, step, way), f_part(dst, step, way), at(dz=way))

    def f_wait(step):
        for way in (1, -1):
            arrived(("f", way, step), f_part((-way * step) % nz, step, way))

    f_send(1)

    id_rows = ids_ref[...]
    marks = jnp.zeros((16, block), f32)
    mrow = lax.broadcasted_iota(i32, (16, block), 0)
    for e in range(EXP_DEV):
        hit = jnp.where(id_rows == ep * EXP_DEV + e, 1.0, 0.0)
        hit = jnp.sum(hit, axis=0, keepdims=True)
        marks = jnp.where(mrow == e, hit, marks)
    earlier = (ri < ci).astype(f32).astype(bf16)
    before = matmul(marks.astype(bf16), earlier)
    srow = lax.broadcasted_iota(i32, (SLOTS, block), 0).astype(f32)
    for e in range(EXP_DEV):
        chosen = (before[e : e + 1, :] == srow) & (marks[e : e + 1, :] > 0.5)
        onehot_ref[e * SLOTS : (e + 1) * SLOTS, :] = jnp.where(chosen, 1.0, 0.0).astype(bf16)

    f_wait(1)
    f_send(2)

    arrived(("w", 1), w_rows(xj(-1)))
    copy(("w2", 1), w_rows(xj(-1), 0, wsplit), w_rows(xj(-1), 0, wsplit), at(dx=1))
    copy(("ws", 1), w_rows(xj(-1)), w_rows(xj(-1)), at(flip=True))
    arrived(("w", -1), w_rows(xj(1)))
    copy(("w2", -1), w_rows(xj(1), wsplit), w_rows(xj(1), wsplit), at(dx=-1))
    copy(("ws", -1), w_rows(xj(1)), w_rows(xj(1)), at(flip=True))

    for step in range(3, half_z + 1):
        f_wait(step - 1)
        f_send(step)

    arrived(("w2", 1), w_rows(xj(2), 0, wsplit))
    copy(("ws2", 1), w_rows(xj(2), 0, wsplit), w_rows(xj(2), 0, wsplit), at(flip=True))
    arrived(("w2", -1), w_rows(xj(2), wsplit))
    copy(("ws2", -1), w_rows(xj(2), wsplit), w_rows(xj(2), wsplit), at(flip=True))

    rb_ref[j] = rt_ref[j]
    for k in range(1, GROUP):
        arrived(("r", k), rb_ref.at[(j + GROUP - k) % GROUP])
    residual = jnp.concatenate(
        [rb_ref[g].astype(f32)[:, :cols] for g in range(GROUP)], axis=1
    )

    own_w.wait()
    arrived(("ws", 0), w_rows(xj_other(0)))
    arrived(("ws", 1), w_rows(xj_other(-1)))
    arrived(("ws", -1), w_rows(xj_other(1)))
    arrived(("ws2", 1), w_rows(xj_other(2), 0, wsplit))
    arrived(("ws2", -1), w_rows(xj_other(2), wsplit))
    f_wait(half_z)

    feats = feat_ref[...].reshape(nz * toks, heads * vdim)
    for lo in range(0, cz, 256):
        hi = min(cz, lo + 256)
        prod = matmul(feats, w_ref[lo:hi, :], NT)
        part_ref[:, lo:hi] = prod
        part16_ref[:, lo:hi] = prod.astype(bf16)

    def part_rows(ref, dy):
        slot = (y + dy - z + nz) % nz
        return ref.at[pl.ds(pl.multiple_of(slot * toks, 16), toks), :]

    for d in range(1, ny):
        copy(("p", d), part_rows(part16_ref, d), got_ref.at[d - 1], at(dy=d))
    total = residual
    own = part_rows(part_ref, 0)[...]
    for d in range(1, ny):
        arrived(("p", d), got_ref.at[d - 1])
        own = own + got_ref[d - 1].astype(f32)
    hidden = (total + own).astype(bf16)

    zsplit = (cz // 128 + 1) // 2 * 128
    xsplit = width // 2

    def z_cols(dz, lo=0, hi=None):
        hi = cz if hi is None else hi
        return pl.ds(pl.multiple_of(((z + dz + nz) % nz) * cz + lo, 128), hi - lo)

    def xx(dx):
        return (x + dx + NX) % NX

    h_ref[x, core, 0, :, z_cols(0)] = hidden[:16]
    h_ref[x, core, 1, :, z_cols(0)] = hidden[16:]

    def piece(way):
        return (0, zsplit) if way > 0 else (zsplit, cz)

    def a1(step, way, cc=core):
        lo, hi = piece(way) if step == half_z else (0, cz)
        return lambda dz: h_ref.at[x, cc, 0, :, z_cols(dz, lo, hi)]

    def a1_send(step):
        for way in (1, -1):
            s = a1(step, way)(-way * (step - 1))
            copy(("a1", way, step), s, s, at(dz=way))

    def a1_wait(step):
        for way in (1, -1):
            arrived(("a1", way, step), a1(step, way)(-way * step))

    def b2(step, way, cc):
        lo, hi = piece(way) if step == half_z else (0, cz)
        return lambda dz: h_ref.at[:, cc, 1, :, z_cols(dz, lo, hi)]

    def b2_send(step):
        for way in (1, -1):
            s = b2(step, way, core)(-way * (step - 1))
            copy(("b2", way, step), s, s, at(dz=way))

    def b2_wait(step):
        for way in (1, -1):
            s = b2(step, way, core)(-way * step)
            arrived(("b2", way, step), s)
            copy(("bs", way, step), s, s, at(flip=True))

    def b1(dx, lo=0, hi=None):
        return h_ref.at[xx(dx), core, 1, :, z_cols(0, lo, hi)]

    def a2(dx, cc, lo=0, hi=None):
        hi = width if hi is None else hi
        return h_ref.at[xx(dx), cc, 0, :, lo:hi]

    a1_send(1)
    for way in (1, -1):
        copy(("b1", way), b1(0), b1(0), at(dx=way))
    for way in (1, -1):
        arrived(("b1", way), b1(-way))
        s = b1(-way, *piece(way))
        copy(("b1r", way), s, s, at(dx=way))
    a1_wait(1)
    a1_send(2)
    for way in (1, -1):
        arrived(("b1r", way), b1(-2 * way, *piece(way)))
    b2_send(1)
    s = b2(0, 1, core)(0)
    copy(("bs", 0), s, s, at(flip=True))
    for step in range(3, half_z + 1):
        a1_wait(step - 1)
        a1_send(step)
    a1_wait(half_z)
    for way in (1, -1):
        copy(("a2", way), a2(0, core), a2(0, core), at(dx=way))
    copy(("as", 0), a2(0, core), a2(0, core), at(flip=True))
    b2_wait(1)
    b2_send(2)

    def x_half(way):
        return (0, xsplit) if way > 0 else (xsplit, width)

    for way in (1, -1):
        arrived(("a2", way), a2(-way, core))
        s = a2(-way, core, *x_half(way))
        copy(("a2r", way), s, s, at(dx=way))
        s = a2(-way, core)
        copy(("as", way), s, s, at(flip=True))
    for step in range(3, half_z + 1):
        b2_wait(step - 1)
        b2_send(step)
    for way in (1, -1):
        s = a2(-2 * way, core, *x_half(way))
        arrived(("a2r", way), s)
        copy(("as2", way), s, s, at(flip=True))
    b2_wait(half_z)

    other = 1 - core
    arrived(("bs", 0), b2(0, 1, other)(0))
    arrived(("as", 0), a2(0, other))
    for way in (1, -1):
        arrived(("as", way), a2(-way, other))
        arrived(("as2", way), a2(-2 * way, other, *x_half(way)))
        for step in range(1, half_z + 1):
            arrived(("bs", way, step), b2(step, way, other)(-way * step))

    si = lax.broadcasted_iota(i32, (cols, cz), 0)
    sc = lax.broadcasted_iota(i32, (cols, cz), 1)
    mine = (sc == si + j * cols).astype(f32).astype(bf16)
    hz = h_ref[:, :, :, :, z_cols(0)].reshape(block, cz)
    hid_ref[...] = matmul(mine, hz, NT).astype(bf16)

    chosen = onehot_ref[...]
    squares = jnp.zeros((EXP_DEV * SLOTS, 1), f32)
    for g in range(nz):
        rows_in = h_ref[:, :, :, :, g * cz : (g + 1) * cz].reshape(block, cz)
        got = matmul(chosen, rows_in)
        picked_ref[:, g * cz : (g + 1) * cz] = got
        squares = squares + jnp.sum(got * got, axis=-1, keepdims=True)
    scale = lax.rsqrt(squares / width + norm_eps)
    for g in range(nz):
        c = slice(g * cz, (g + 1) * cz)
        out_ref[:, c] = (picked_ref[:, c] * scale * gain_ref[:, c]).astype(bf16)

    for c in sends:
        c.wait_send()
    assert len(ids.names) <= sem_count


def shards(
    queries,
    trunk_cache,
    branch_cache,
    visible,
    branch_len,
    value_up,
    out_proj,
    residual_in,
    norm_gain,
    expert_ids,
):
    ny = lax.axis_size("narrow")
    nz = lax.axis_size("ep") // GROUP
    trees, branches = branch_len.shape
    heads, lat, vdim = value_up.shape
    kdim = queries.shape[2]
    trunk_len = trunk_cache.shape[1]
    nkeys = branches * branch_cache.shape[2]
    feat, cols = out_proj.shape
    block = residual_in.shape[0]
    toks = trees * branches
    rows = branches * heads
    cz = GROUP * cols
    width = nz * cz
    bf16, f32 = jnp.bfloat16, jnp.float32
    sem_count = 96
    hbm = pl.BlockSpec(memory_space=pl.ANY)
    vmem = pl.BlockSpec(memory_space=pltpu.VMEM)
    chosen = EXP_DEV * SLOTS
    hidden, rows_out = pl.pallas_call(
        functools.partial(kernel, (ny, nz, sem_count)),
        out_shape=(
            jax.ShapeDtypeStruct((cols, block), bf16),
            jax.ShapeDtypeStruct((chosen, width), bf16),
        ),
        in_specs=[hbm] * 5 + [vmem] * 5,
        out_specs=(vmem, vmem),
        scratch_shapes=[
            pltpu.VMEM((trees, rows, kdim), bf16),
            pltpu.VMEM((trees, kdim, trunk_len), bf16),
            pltpu.VMEM((trees, nkeys, kdim), bf16),
            pltpu.VMEM((heads, lat, vdim), bf16),
            pltpu.VMEM((rows, trunk_len + nkeys), f32),
            pltpu.VMEM((rows, trunk_len + nkeys), bf16),
            pltpu.VMEM((branches, nkeys), f32),
            pltpu.VMEM((heads, toks, lat), bf16),
            pltpu.VMEM((nz, toks, feat), bf16),
            pltpu.VMEM((cz, feat), bf16),
            pltpu.VMEM((GROUP, toks, 128), bf16),
            pltpu.VMEM((GROUP, toks, 128), bf16),
            pltpu.VMEM((nz * toks, cz), f32),
            pltpu.VMEM((nz * toks, cz), bf16),
            pltpu.VMEM((ny - 1, toks, cz), bf16),
            pltpu.VMEM((NX, 2, 2, 16, width), bf16),
            pltpu.VMEM((chosen, block), bf16),
            pltpu.VMEM((chosen, width), f32),
            pltpu.SemaphoreType.DMA((16,)),
            pltpu.SemaphoreType.DMA((sem_count,)),
            pltpu.SemaphoreType.DMA((sem_count,)),
        ],
        compiler_params=pltpu.CompilerParams(
            collective_id=0, has_side_effects=True, vmem_limit_bytes=48 * 1024 * 1024
        ),
        name="decode_layer",
    )(
        queries.reshape(trees, rows, kdim),
        jnp.swapaxes(trunk_cache, 1, 2),
        branch_cache.reshape(trees, nkeys, kdim),
        value_up,
        out_proj.T,
        visible,
        branch_len,
        residual_in.T,
        norm_gain.reshape(1, width),
        expert_ids.T,
    )
    return hidden.T, rows_out.reshape(1, EXP_DEV, SLOTS, width)


def solution(mesh):
    placed = (
        P("ep", "narrow", None),
        P("ep", None, None),
        P("ep", None, None, None),
        P("ep", None, None),
        P("ep", None),
        P("narrow", None, None),
        P("narrow", "ep"),
        P("narrow", "ep"),
        P(),
        P("narrow", None),
    )
    return jax.shard_map(
        shards,
        mesh=mesh,
        in_specs=placed,
        out_specs=(P("narrow", "ep"), P("narrow", "ep", None, None)),
        check_vma=False,
    )
```

time: 343 us -> 97.5 us (0.28)
  blocking collectives: 159 us -> 0 us
  waiting for transfers between devices: 95.2 us -> 0 us
  Pallas kernels: 0 us -> 86.2 us
  other arithmetic: 41.2 us -> 0 us
  matrix products: 17.2 us -> 0 us
  between operations: 14.2 us -> 0.66 us
  local copies, waits for them, and re-layouts: 15.2 us -> 10.1 us
    psum x1 -> x0, blocking collectives: 124 us -> none  [shards(): total_squares = lax.psum(local_squares, 'ep')]
    all_gather x1 -> x0, waiting for transfers between devices: 95.1 us -> none  [shards(): lax.all_gather(features, 'ep', axis=0, tiled=True)]
    pallas_call x0 -> x1, Pallas kernels: none -> 86.2 us  [shards(): pl.pallas_call(functools.partial(kernel, (ny, nz, sem_count)), out_shape=...]
    reduce_or x1 -> x0, other arithmetic: 37.4 us -> none  [shards(): jnp.any(target[None, :, :] == jnp.arange(experts * slots, dtype=jnp.int32...]
    all_to_all x1 -> x0, blocking collectives: 35.4 us -> none  [shards(): lax.all_to_all(outgoing, 'ep', split_axis=0, concat_axis=3, tiled=True)]
    dot_general x8 -> x0, matrix products: 17.2 us -> none  [the longest x1 7.12 us: shards(): jnp.dot(lax.all_gather(features, 'ep', axis=0, tiled=True), out_proj, pre...]
    unnamed x11 -> x20, local copies, waits for them, and re-layouts: 0.8 us -> 10.1 us
    all_to_all x2 -> x0, local copies, waits for them, and re-layouts: 3.86 us -> none  [shards(): lax.all_to_all(outgoing, 'ep', split_axis=0, concat_axis=3, tiled=True)]
  transfers between devices with their start and end apart: 2 -> 0, of which waited for: 1 -> 0; matrix products, arithmetic and copies ran while one was open for 12% -> 0% of each run, Pallas kernels for 0% -> 0%
where the time goes in v1:
time: 97.5 us; the launch traced here: 97 us
  Pallas kernels  86.2 us (88%)
  local copies, waits for them, and re-layouts  10.1 us (10%)
    pallas_call x1, Pallas kernels, shards(): pl.pallas_call(functools.partial(kernel, (ny, nz, sem_count)), out_shape=...  86.2 us
    unnamed x20, local copies, waits for them, and re-layouts  10.1 us

profile of v1, /device:TPU:1, one launch (start us, length us, event | category | flops | bytes accessed | tf_op | source)
XLA Modules:
  0.0 97.0 jit_solution(2239930224991833276)
XLA Ops:
  0.6 0.0 copy-start
  0.6 1.5 %copy-done = bf16[2,768,576]{1,2,0:T(8,128)(2,1)S(1)} copy-done((bf16[2,768,576]{1,2,0:T(8,128)(2,1)S(1)}, bf16[2,768,576]{1,2,0:T(8,128)(2,1)}, u32[]{:S(2)}) %copy-start) | copy-done | bytes 1769496
  2.1 0.0 copy-start.1
  2.1 1.3 %copy-done.1 = bf16[2,16,32,576]{3,2,1,0:T(8,128)(2,1)S(1)} copy-done((bf16[2,16,32,576]{3,2,1,0:T(8,128)(2,1)S(1)}, bf16[2,16,32,576]{3,2,1,0:T(8,128)(2,1)}, u32[]{:S(2)}) %copy-start.1) | copy-done | bytes 1179672
  3.4 0.0 copy-start.2
  3.4 1.1 %copy-done.2 = bf16[32,16,576]{2,1,0:T(8,128)(2,1)S(1)} copy-done((bf16[32,16,576]{2,1,0:T(8,128)(2,1)S(1)}, bf16[32,16,576]{2,1,0:T(8,128)(2,1)}, u32[]{:S(2)}) %copy-start.2) | copy-done | bytes 589848
  4.5 0.0 copy-start.3
  4.5 1.0 %copy-done.3 = bf16[2048,112]{0,1:T(8,128)(2,1)S(1)} copy-done((bf16[2048,112]{0,1:T(8,128)(2,1)S(1)}, bf16[2048,112]{0,1:T(8,128)(2,1)}, u32[]{:S(2)}) %copy-start.3) | copy-done | bytes 458776
  5.5 0.0 copy-start.4
  5.5 0.8 copy-done.4
  6.4 0.0 copy-start.5
  6.4 0.7 copy-done.5
  7.1 0.0 copy-start.6
  7.1 0.7 copy-done.6
  7.8 0.0 copy-start.7
  7.8 0.7 copy-done.7
  8.5 0.0 copy-start.8
  8.5 0.7 copy-done.8
  9.2 86.2 %decode_layer.1 = (bf16[112,256]{1,0:T(8,128)(2,1)S(1)}, bf16[64,7168]{1,0:T(8,128)(2,1)S(1)}) custom-call(bf16[2,256,576]{2,1,0:T(8,128)(2,1)S(1)} %bitcast.12, bf16[2,576,768]{2,1,0:T(8,128)(2,1)S(1)} %bitcast.9, bf16[2,512,576]{2,1,0:T(8,128)(2,1)S(1)} %bitcast.10, bf16[16,512,128]{2,1,0:T(8,128)(2,1)} %vup_hbm.1, bf16[112,2048]{1,0:T(8,128)(2,1)S(1)} %bitcast.13, ...), custom_call_target="tpu_custom_call" | custom-call | tf_op jit(solution)/shard_map/decode_layer/pallas_call | solution.py:475
  95.4 0.6 copy.14
  96.1 0.9 copy.15
Async XLA Ops:
  0.6 1.5 %copy-start = (bf16[2,768,576]{1,2,0:T(8,128)(2,1)S(1)}, bf16[2,768,576]{1,2,0:T(8,128)(2,1)}, u32[]{:S(2)}) copy-start(bf16[2,768,576]{1,2,0:T(8,128)(2,1)} %param.11) | copy-start | bytes 5308420
  2.1 1.3 %copy-start.1 = (bf16[2,16,32,576]{3,2,1,0:T(8,128)(2,1)S(1)}, bf16[2,16,32,576]{3,2,1,0:T(8,128)(2,1)}, u32[]{:S(2)}) copy-start(bf16[2,16,32,576]{3,2,1,0:T(8,128)(2,1)} %param.12) | copy-start | bytes 3538948
  3.4 1.1 %copy-start.2 = (bf16[32,16,576]{2,1,0:T(8,128)(2,1)S(1)}, bf16[32,16,576]{2,1,0:T(8,128)(2,1)}, u32[]{:S(2)}) copy-start(bf16[32,16,576]{2,1,0:T(8,128)(2,1)} %param.10) | copy-start | bytes 1769476
  4.5 1.0 %copy-start.3 = (bf16[2048,112]{0,1:T(8,128)(2,1)S(1)}, bf16[2048,112]{0,1:T(8,128)(2,1)}, u32[]{:S(2)}) copy-start(bf16[2048,112]{0,1:T(8,128)(2,1)} %param.16) | copy-start | bytes 1376260
  5.5 0.8 copy-start.4
  6.4 0.7 copy-start.5
  7.1 0.7 copy-start.6
  7.8 0.7 copy-start.7
  8.5 0.7 copy-start.8

commit v2 on v1

v2 whole, which is shorter than its diff:
```python
import functools

import jax
import jax.numpy as jnp
from jax import lax
from jax.experimental import pallas as pl
from jax.experimental.pallas import tpu as pltpu
from jax.sharding import PartitionSpec as P

NX = 4
GROUP = 2 * NX
EXP_DEV = 4
SLOTS = 16

score_scale = 192.0 ** (-0.5)
norm_eps = 1e-06

MESH = pl.DeviceIdType.MESH
NT = (((1,), (1,)), ((), ()))
NN = (((1,), (0,)), ((), ()))


def matmul(a, b, dims=NN):
    return lax.dot_general(a, b, dims, preferred_element_type=jnp.float32)


class Ids:
    def __init__(self):
        self.names = {}

    def __call__(self, *name):
        return self.names.setdefault(name, len(self.names))


def kernel(
    cfg,
    q_hbm,
    trunk_hbm,
    branch_hbm,
    vup_hbm,
    w_hbm,
    vis_hbm,
    len_hbm,
    res_hbm,
    gain_hbm,
    ids_hbm,
    hid_ref,
    out_ref,
    q_ref,
    trunk_ref,
    branch_ref,
    vup_ref,
    vis_ref,
    len_ref,
    res_ref,
    gain_ref,
    ids_ref,
    s_ref,
    p_ref,
    bias_ref,
    lat_ref,
    feat_ref,
    w_ref,
    rt_ref,
    rb_ref,
    part_ref,
    part16_ref,
    got_ref,
    sum_ref,
    h_ref,
    onehot_ref,
    picked_ref,
    in_sem,
    send_sem,
    recv_sem,
):
    ny, nz, sem_count = cfg
    trees, rows, kdim = q_ref.shape
    trunk_len = trunk_ref.shape[2]
    nkeys = branch_ref.shape[1]
    heads, lat, vdim = vup_ref.shape
    branches = vis_ref.shape[1]
    brmost = nkeys // branches
    cols = w_hbm.shape[0]
    cz = GROUP * cols
    toks = trees * branches
    block = GROUP * toks
    width = nz * cz
    bf16, f32, i32 = jnp.bfloat16, jnp.float32, jnp.int32
    REL = [0] + [w * d for d in range(1, nz // 2) for w in (1, -1)] + [nz // 2]
    near = 5

    def slot(rel):
        return REL.index(rel if rel in REL else (rel % nz))

    y = lax.axis_index("narrow")
    ep = lax.axis_index("ep")
    z = ep // GROUP
    j = ep % GROUP
    x = j // 2
    core = j % 2

    def at(dy=0, dz=0, dx=0, flip=False):
        yy = (y + dy + ny) % ny
        zz = (z + dz + nz) % nz
        xx = (x + dx + NX) % NX
        cc = 1 - core if flip else core
        return (yy, zz * GROUP + xx * 2 + cc)

    barrier = pltpu.get_barrier_semaphore()
    partners = [at(dz=1), at(dz=-1), at(dz=2), at(dz=-2)]
    partners += [(y, z * GROUP + (j + k) % GROUP) for k in range(1, GROUP)]
    partners += [at(dy=d) for d in range(1, ny)]
    for p in partners:
        pl.semaphore_signal(barrier, inc=1, device_id=p, device_id_type=MESH)

    loads = []

    def load(src, dst):
        c = pltpu.make_async_copy(src, dst, in_sem.at[len(loads)])
        c.start()
        loads.append(c)
        return c

    def w_rows(jj):
        return w_ref.at[pl.ds(pl.multiple_of(jj * cols, 16), cols), :]

    res_load = load(res_hbm, res_ref)
    mask_loads = [load(vis_hbm, vis_ref), load(len_hbm, len_ref)]
    tree_loads = []
    for t in range(trees):
        tree_loads.append(
            [
                load(q_hbm.at[t], q_ref.at[t]),
                load(trunk_hbm.at[t], trunk_ref.at[t]),
                load(branch_hbm.at[t], branch_ref.at[t]),
            ]
        )
    vup_load = load(vup_hbm, vup_ref)
    own_w = load(w_hbm, w_rows(j))
    late_loads = [load(ids_hbm, ids_ref), load(gain_hbm, gain_ref)]

    sends = []
    ids = Ids()

    def copy(name, src, dst, dev):
        i = ids(*name)
        c = pltpu.make_async_remote_copy(
            src_ref=src,
            dst_ref=dst,
            send_sem=send_sem.at[i],
            recv_sem=recv_sem.at[i],
            device_id=dev,
            device_id_type=MESH,
        )
        c.start()
        sends.append(c)

    def arrived(name, dst):
        i = ids(*name)
        pltpu.make_async_remote_copy(
            src_ref=dst,
            dst_ref=dst,
            send_sem=send_sem.at[i],
            recv_sem=recv_sem.at[i],
            device_id=at(flip=True),
            device_id_type=MESH,
        ).wait_recv()

    pl.semaphore_wait(barrier, len(partners))

    def xj(dx):
        return ((x + dx + NX) % NX) * 2 + core

    def xj_other(dx):
        return ((x + dx + NX) % NX) * 2 + (1 - core)

    for d in (1, -1, 2):
        copy(("w", d), w_hbm, w_rows(j), at(dx=d))
    copy(("ws", 0), w_hbm, w_rows(j), at(flip=True))

    res_load.wait()
    res = res_ref[...]
    fill = 128 - cols
    if fill:
        res = jnp.concatenate([res, jnp.zeros((fill, block), bf16)], axis=0)
    ri = lax.broadcasted_iota(i32, (block, block), 0)
    ci = lax.broadcasted_iota(i32, (block, block), 1)
    eye = (ri == ci).astype(f32).astype(bf16)
    rt_ref[...] = matmul(eye, res, NT).astype(bf16).reshape(GROUP, toks, 128)
    for k in range(1, GROUP):
        jj = (j + k) % GROUP
        copy(("r", k), rt_ref.at[jj], rb_ref.at[j], (y, z * GROUP + jj))

    def z_first(name, part):
        for d in (2, 1):
            for way in (1, -1):
                copy((name, -way * d), part(0, None), part(slot(-way * d), None), at(dz=way * d))

    def z_second(name, part):
        for way in (1, -1):
            arrived((name, -2 * way), part(slot(-2 * way), None))
            src = slot(-2 * way)
            copy((name, -3 * way), part(src, None), part(slot(-3 * way), None), at(dz=way))
            copy((name, 4, way), part(src, way), part(slot(4), way), at(dz=2 * way))

    def z_near(name, part):
        for way in (1, -1):
            arrived((name, -way), part(slot(-way), None))

    def z_far(name, part):
        for way in (1, -1):
            arrived((name, -3 * way), part(slot(-3 * way), None))
            arrived((name, 4, way), part(slot(4), way))

    feat = heads * vdim

    def f_part(t):
        def part(s, way):
            c = slice(None) if way is None else slice(0, feat // 2) if way > 0 else slice(feat // 2, feat)
            return feat_ref.at[s, t * branches : (t + 1) * branches, c]

        return part

    ro = lax.broadcasted_iota(i32, (rows, rows), 0)
    co = lax.broadcasted_iota(i32, (rows, rows), 1)
    swap = (co == (ro % branches) * heads + ro // branches).astype(f32).astype(bf16)
    for c in mask_loads:
        c.wait()
    for t in range(trees):
        key_i = lax.broadcasted_iota(i32, (branches, nkeys), 1)
        owner = key_i // brmost
        pos = key_i % brmost
        vis = jnp.zeros((branches, nkeys), i32)
        lim = jnp.zeros((branches, nkeys), i32)
        for b in range(branches):
            here = owner == b
            vis = jnp.where(here, vis_ref[t, :, b : b + 1], vis)
            lim = jnp.where(here, len_ref[t : t + 1, b : b + 1], lim)
        live = (vis > 0) & (pos < lim)
        bias_ref[...] = jnp.where(live, 0.0, -1e30)

        for c in tree_loads[t]:
            c.wait()
        q = q_ref[t]
        s_ref[:, :trunk_len] = matmul(q, trunk_ref[t])
        s_ref[:, trunk_len:] = matmul(q, branch_ref[t], NT)

        def soft(b, carry):
            r = pl.ds(pl.multiple_of(b * heads, heads), heads)
            st = s_ref[r, :trunk_len] * score_scale
            sb = s_ref[r, trunk_len:] * score_scale + bias_ref[pl.ds(b, 1), :]
            top = jnp.maximum(
                jnp.max(st, axis=-1, keepdims=True), jnp.max(sb, axis=-1, keepdims=True)
            )
            et = jnp.exp(st - top)
            eb = jnp.exp(sb - top)
            inv = 1.0 / (
                jnp.sum(et, axis=-1, keepdims=True) + jnp.sum(eb, axis=-1, keepdims=True)
            )
            p_ref[r, :trunk_len] = (et * inv).astype(bf16)
            p_ref[r, trunk_len:] = (eb * inv).astype(bf16)
            return carry

        lax.fori_loop(0, branches, soft, 0, unroll=4)
        o = matmul(p_ref[:, :trunk_len], trunk_ref[t, :lat, :], NT)
        o = o + matmul(p_ref[:, trunk_len:], branch_ref[t, :, :lat])
        o = matmul(swap, o.astype(bf16)).astype(bf16)
        lat_ref[...] = o.reshape(heads, branches, lat)
        if t == 0:
            vup_load.wait()
        for h in range(heads):
            f = matmul(lat_ref[h], vup_ref[h])
            feat_ref[0, t * branches : (t + 1) * branches, h * vdim : (h + 1) * vdim] = f.astype(bf16)
        z_first("f%d" % t, f_part(t))

    for c in late_loads:
        c.wait()
    id_rows = ids_ref[...]
    marks = jnp.zeros((16, block), f32)
    mrow = lax.broadcasted_iota(i32, (16, block), 0)
    for e in range(EXP_DEV):
        hit = jnp.where(id_rows == ep * EXP_DEV + e, 1.0, 0.0)
        hit = jnp.sum(hit, axis=0, keepdims=True)
        marks = jnp.where(mrow == e, hit, marks)
    earlier = (ri < ci).astype(f32).astype(bf16)
    before = matmul(marks.astype(bf16), earlier)
    srow = lax.broadcasted_iota(i32, (SLOTS, block), 0).astype(f32)
    for e in range(EXP_DEV):
        chosen = (before[e : e + 1, :] == srow) & (marks[e : e + 1, :] > 0.5)
        onehot_ref[e * SLOTS : (e + 1) * SLOTS, :] = jnp.where(chosen, 1.0, 0.0).astype(bf16)

    z_second("f0", f_part(0))
    for d in (1, -1):
        arrived(("w", d), w_rows(xj(-d)))
        copy(("ws", d), w_rows(xj(-d)), w_rows(xj(-d)), at(flip=True))
    for t in range(1, trees):
        z_second("f%d" % t, f_part(t))

    rb_ref[j] = rt_ref[j]
    for k in range(1, GROUP):
        arrived(("r", k), rb_ref.at[(j + GROUP - k) % GROUP])
    residual = jnp.concatenate(
        [rb_ref[g].astype(f32)[:, :cols] for g in range(GROUP)], axis=1
    )
    sum_ref[...] = residual

    arrived(("w", 2), w_rows(xj(2)))
    copy(("ws", 2), w_rows(xj(2)), w_rows(xj(2)), at(flip=True))
    own_w.wait()
    for d in (0, 1, -1, 2):
        arrived(("ws", d), w_rows(xj_other(-d)))
    for t in range(trees):
        z_near("f%d" % t, f_part(t))

    p_ids = [ids("p", d) for d in range(1, ny)]
    assert p_ids[-1] - p_ids[0] == ny - 2

    def part_copy(s, d):
        return pltpu.make_async_remote_copy(
            src_ref=part16_ref.at[s],
            dst_ref=got_ref.at[d - 1],
            send_sem=send_sem.at[p_ids[0] + d - 1],
            recv_sem=recv_sem.at[p_ids[0] + d - 1],
            device_id=at(dy=d),
            device_id_type=MESH,
        )

    def project(first, last):
        feats = feat_ref[first:last].reshape((last - first) * toks, feat)
        for lo in range(0, cz, 256):
            hi = min(cz, lo + 256)
            prod = matmul(feats, w_ref[lo:hi, :], NT).reshape(last - first, toks, hi - lo)
            part_ref[first:last, :, lo:hi] = prod
            part16_ref[first:last, :, lo:hi] = prod.astype(bf16)
        for s in range(first, last):
            d = (z + REL[s] - y + 2 * ny) % ny

            @pl.when(d != 0)
            def _():
                part_copy(s, d).start()

    project(0, near)
    for t in range(trees):
        z_far("f%d" % t, f_part(t))
    project(near, nz)
    dz_own = (y - z + nz) % nz
    own_slot = jnp.maximum(
        0, 2 * jnp.minimum(dz_own, nz - dz_own) - 1 + (dz_own > nz // 2).astype(i32)
    )
    total = part_ref[own_slot]
    for d in range(1, ny):
        arrived(("p", d), got_ref.at[d - 1])
        total = total + got_ref[d - 1].astype(f32)
    hidden = (sum_ref[...] + total).astype(bf16)

    ca = max(1, (cz * 5 // 7) // 128) * 128
    h_ref[0, x, core] = hidden

    def row_half(way):
        if way is None:
            return slice(None)
        return slice(0, toks // 2) if way > 0 else slice(toks // 2, toks)

    def a1(s, way):
        return h_ref.at[s, x, core, row_half(way), :ca]

    def b2(s, way):
        return h_ref.at[s, :, core, row_half(way), ca:]

    def b1(dx):
        return h_ref.at[0, (x + dx + NX) % NX, core, :, ca:]

    parts_z = ((0, 1), (1, near), (near, nz))

    def a2(g, dx):
        return h_ref.at[parts_z[g][0] : parts_z[g][1], (x + dx + NX) % NX, core, :, :ca]

    def a2_send(g):
        for d in (2, 1, -1):
            copy(("a2", g, d), a2(g, 0), a2(g, 0), at(dx=d))

    def a2_take(g):
        for d in (1, -1, 2):
            arrived(("a2", g, d), a2(g, -d))
        s = h_ref.at[parts_z[g][0] : parts_z[g][1], :, core, :, :ca]
        copy(("as", g), s, s, at(flip=True))

    def b_share(g):
        s = h_ref.at[parts_z[g][0] : parts_z[g][1], :, core, :, ca:]
        copy(("bs", g), s, s, at(flip=True))

    def shared(g):
        c = slice(parts_z[g][0], parts_z[g][1])
        arrived(("as", g), h_ref.at[c, :, 1 - core, :, :ca])
        arrived(("bs", g), h_ref.at[c, :, 1 - core, :, ca:])

    for d in (2, 1, -1):
        copy(("b1", d), b1(0), b1(0), at(dx=d))
    z_first("a1", a1)
    a2_send(0)
    for d in (1, -1, 2):
        arrived(("b1", d), b1(-d))
    z_first("b2", b2)
    b_share(0)
    z_second("a1", a1)
    z_near("a1", a1)
    a2_send(1)
    a2_take(0)
    z_second("b2", b2)
    z_near("b2", b2)
    b_share(1)
    z_far("a1", a1)
    a2_send(2)
    a2_take(1)
    shared(0)

    si = lax.broadcasted_iota(i32, (cols, cz), 0)
    sc = lax.broadcasted_iota(i32, (cols, cz), 1)
    mine = (sc == si + j * cols).astype(f32).astype(bf16)
    hid_ref[...] = matmul(mine, h_ref[0].reshape(block, cz), NT).astype(bf16)

    def pick(g, squares):
        for s in range(*parts_z[g]):
            got = matmul(onehot_ref[...], h_ref[s].reshape(block, cz))
            picked_ref[s] = got
            squares = squares + jnp.sum(got * got, axis=-1, keepdims=True)
        return squares

    squares = pick(0, jnp.zeros((EXP_DEV * SLOTS, 1), f32))
    z_far("b2", b2)
    b_share(2)
    shared(1)
    squares = pick(1, squares)
    a2_take(2)
    shared(2)
    squares = pick(2, squares)
    scale = lax.rsqrt(squares / width + norm_eps)
    for s in range(nz):
        at_z = pl.ds(pl.multiple_of(((z + REL[s] + nz) % nz) * cz, 128), cz)
        out_ref[:, at_z] = (picked_ref[s] * scale * gain_ref[:, at_z]).astype(bf16)

    for d in range(1, ny):
        part_copy(0, d).wait_send()
    for c in sends:
        c.wait_send()
    assert len(ids.names) <= sem_count


def shards(
    queries,
    trunk_cache,
    branch_cache,
    visible,
    branch_len,
    value_up,
    out_proj,
    residual_in,
    norm_gain,
    expert_ids,
):
    ny = lax.axis_size("narrow")
    nz = lax.axis_size("ep") // GROUP
    trees, branches = branch_len.shape
    heads, lat, vdim = value_up.shape
    kdim = queries.shape[2]
    trunk_len = trunk_cache.shape[1]
    nkeys = branches * branch_cache.shape[2]
    feat, cols = out_proj.shape
    block = residual_in.shape[0]
    toks = trees * branches
    rows = branches * heads
    cz = GROUP * cols
    width = nz * cz
    bf16, f32 = jnp.bfloat16, jnp.float32
    sem_count = 96
    hbm = pl.BlockSpec(memory_space=pl.ANY)
    vmem = pl.BlockSpec(memory_space=pltpu.VMEM)
    chosen = EXP_DEV * SLOTS
    hidden, rows_out = pl.pallas_call(
        functools.partial(kernel, (ny, nz, sem_count)),
        out_shape=(
            jax.ShapeDtypeStruct((cols, block), bf16),
            jax.ShapeDtypeStruct((chosen, width), bf16),
        ),
        in_specs=[hbm] * 10,
        out_specs=(vmem, vmem),
        scratch_shapes=[
            pltpu.VMEM((trees, rows, kdim), bf16),
            pltpu.VMEM((trees, kdim, trunk_len), bf16),
            pltpu.VMEM((trees, nkeys, kdim), bf16),
            pltpu.VMEM((heads, lat, vdim), bf16),
            pltpu.VMEM(visible.shape, jnp.int32),
            pltpu.VMEM(branch_len.shape, jnp.int32),
            pltpu.VMEM((cols, block), bf16),
            pltpu.VMEM((1, width), f32),
            pltpu.VMEM(expert_ids.shape[::-1], jnp.int32),
            pltpu.VMEM((rows, trunk_len + nkeys), f32),
            pltpu.VMEM((rows, trunk_len + nkeys), bf16),
            pltpu.VMEM((branches, nkeys), f32),
            pltpu.VMEM((heads, branches, lat), bf16),
            pltpu.VMEM((nz, toks, feat), bf16),
            pltpu.VMEM((cz, feat), bf16),
            pltpu.VMEM((GROUP, toks, 128), bf16),
            pltpu.VMEM((GROUP, toks, 128), bf16),
            pltpu.VMEM((nz, toks, cz), f32),
            pltpu.VMEM((nz, toks, cz), bf16),
            pltpu.VMEM((ny - 1, toks, cz), bf16),
            pltpu.VMEM((toks, cz), f32),
            pltpu.VMEM((nz, NX, 2, toks, cz), bf16),
            pltpu.VMEM((chosen, block), bf16),
            pltpu.VMEM((nz, chosen, cz), f32),
            pltpu.SemaphoreType.DMA((16,)),
            pltpu.SemaphoreType.DMA((sem_count,)),
            pltpu.SemaphoreType.DMA((sem_count,)),
        ],
        compiler_params=pltpu.CompilerParams(
            collective_id=0, has_side_effects=True, vmem_limit_bytes=63 * 1024 * 1024
        ),
        name="decode_layer",
    )(
        queries.reshape(trees, rows, kdim),
        jnp.swapaxes(trunk_cache, 1, 2),
        branch_cache.reshape(trees, nkeys, kdim),
        value_up,
        out_proj.T,
        visible,
        branch_len,
        residual_in.T,
        norm_gain.reshape(1, width),
        expert_ids.T,
    )
    return hidden.T, rows_out.reshape(1, EXP_DEV, SLOTS, width)


def solution(mesh):
    placed = (
        P("ep", "narrow", None),
        P("ep", None, None),
        P("ep", None, None, None),
        P("ep", None, None),
        P("ep", None),
        P("narrow", None, None),
        P("narrow", "ep"),
        P("narrow", "ep"),
        P(),
        P("narrow", None),
    )
    return jax.shard_map(
        shards,
        mesh=mesh,
        in_specs=placed,
        out_specs=(P("narrow", "ep"), P("narrow", "ep", None, None)),
        check_vma=False,
    )
```

time: 97.5 us -> 83.2 us (0.85)
  Pallas kernels: 86.2 us -> 78.8 us
  local copies, waits for them, and re-layouts: 10.1 us -> 3.61 us
    pallas_call x1, Pallas kernels: 86.2 us -> 78.8 us  [shards(): pl.pallas_call(functools.partial(kernel, (ny, nz, sem_count)), out_shape=...]
    unnamed x20 -> x2, local copies, waits for them, and re-layouts: 10.1 us -> 3.61 us
where the time goes in v2:
time: 83.2 us; the launch traced here: 83 us
  Pallas kernels  78.8 us (95%)
  local copies, waits for them, and re-layouts  3.61 us (4%)
    pallas_call x1, Pallas kernels, shards(): pl.pallas_call(functools.partial(kernel, (ny, nz, sem_count)), out_shape=...  78.8 us
    unnamed x2, local copies, waits for them, and re-layouts  3.61 us

profile of v2, /device:TPU:1, one launch (start us, length us, event | category | flops | bytes accessed | tf_op | source)
XLA Modules:
  0.0 83.0 jit_solution(8799325645664122007)
XLA Ops:
  0.6 78.8 %decode_layer.1 = (bf16[112,256]{1,0:T(8,128)(2,1)}, bf16[64,7168]{1,0:T(8,128)(2,1)}) custom-call(bf16[2,256,576]{2,1,0:T(8,128)(2,1)} %bitcast.12, bf16[2,576,768]{2,1,0:T(8,128)(2,1)} %bitcast.9, bf16[2,512,576]{2,1,0:T(8,128)(2,1)} %bitcast.10, bf16[16,512,128]{2,1,0:T(8,128)(2,1)} %vup_hbm.1, bf16[112,2048]{1,0:T(8,128)(2,1)} %bitcast.13, ...), custom_call_target="tpu_custom_call" | custom-call | tf_op jit(solution)/shard_map/decode_layer/pallas_call | solution.py:480
  79.4 1.4 %copy.14 = bf16[256,112]{0,1:T(8,128)(2,1)} copy(bf16[256,112]{0,1:T(8,128)(2,1)} %bitcast.15) | data formatting | bytes 114688
  80.8 2.2 %copy.15 = bf16[1,4,16,7168]{3,2,1,0:T(8,128)(2,1)} copy(bf16[1,4,16,7168]{3,2,1,0:T(8,128)(2,1)} %bitcast.11) | data formatting | bytes 1835008

commit v3 on v2

--- a/solution.py
+++ b/solution.py
@@ -122,8 +122,8 @@
         loads.append(c)
         return c
 
-    def w_rows(jj):
-        return w_ref.at[pl.ds(pl.multiple_of(jj * cols, 16), cols), :]
+    def w_rows(jj, lo=0, hi=cols):
+        return w_ref.at[pl.ds(pl.multiple_of(jj * cols + lo, 16), hi - lo), :]
 
     res_load = load(res_hbm, res_ref)
     mask_loads = [load(vis_hbm, vis_ref), load(len_hbm, len_ref)]
@@ -167,64 +167,6 @@
             device_id_type=MESH,
         ).wait_recv()
 
-    pl.semaphore_wait(barrier, len(partners))
-
-    def xj(dx):
-        return ((x + dx + NX) % NX) * 2 + core
-
-    def xj_other(dx):
-        return ((x + dx + NX) % NX) * 2 + (1 - core)
-
-    for d in (1, -1, 2):
-        copy(("w", d), w_hbm, w_rows(j), at(dx=d))
-    copy(("ws", 0), w_hbm, w_rows(j), at(flip=True))
-
-    res_load.wait()
-    res = res_ref[...]
-    fill = 128 - cols
-    if fill:
-        res = jnp.concatenate([res, jnp.zeros((fill, block), bf16)], axis=0)
-    ri = lax.broadcasted_iota(i32, (block, block), 0)
-    ci = lax.broadcasted_iota(i32, (block, block), 1)
-    eye = (ri == ci).astype(f32).astype(bf16)
-    rt_ref[...] = matmul(eye, res, NT).astype(bf16).reshape(GROUP, toks, 128)
-    for k in range(1, GROUP):
-        jj = (j + k) % GROUP
-        copy(("r", k), rt_ref.at[jj], rb_ref.at[j], (y, z * GROUP + jj))
-
-    def z_first(name, part):
-        for d in (2, 1):
-            for way in (1, -1):
-                copy((name, -way * d), part(0, None), part(slot(-way * d), None), at(dz=way * d))
-
-    def z_second(name, part):
-        for way in (1, -1):
-            arrived((name, -2 * way), part(slot(-2 * way), None))
-            src = slot(-2 * way)
-            copy((name, -3 * way), part(src, None), part(slot(-3 * way), None), at(dz=way))
-            copy((name, 4, way), part(src, way), part(slot(4), way), at(dz=2 * way))
-
-    def z_near(name, part):
-        for way in (1, -1):
-            arrived((name, -way), part(slot(-way), None))
-
-    def z_far(name, part):
-        for way in (1, -1):
-            arrived((name, -3 * way), part(slot(-3 * way), None))
-            arrived((name, 4, way), part(slot(4), way))
-
-    feat = heads * vdim
-
-    def f_part(t):
-        def part(s, way):
-            c = slice(None) if way is None else slice(0, feat // 2) if way > 0 else slice(feat // 2, feat)
-            return feat_ref.at[s, t * branches : (t + 1) * branches, c]
-
-        return part
-
-    ro = lax.broadcasted_iota(i32, (rows, rows), 0)
-    co = lax.broadcasted_iota(i32, (rows, rows), 1)
-    swap = (co == (ro % branches) * heads + ro // branches).astype(f32).astype(bf16)
     for c in mask_loads:
         c.wait()
     for t in range(trees):
@@ -238,8 +180,81 @@
             vis = jnp.where(here, vis_ref[t, :, b : b + 1], vis)
             lim = jnp.where(here, len_ref[t : t + 1, b : b + 1], lim)
         live = (vis > 0) & (pos < lim)
-        bias_ref[...] = jnp.where(live, 0.0, -1e30)
-
+        bias_ref[t] = jnp.where(live, 0.0, -1e30)
+
+    pl.semaphore_wait(barrier, len(partners))
+
+    def xj(dx):
+        return ((x + dx + NX) % NX) * 2 + core
+
+    def xj_other(dx):
+        return ((x + dx + NX) % NX) * 2 + (1 - core)
+
+    w_cut = (cols // 16 + 1) // 2 * 16
+
+    def w_part(way, first):
+        return (0, w_cut) if (way > 0) == first else (w_cut, cols)
+
+    def w_send(way, first):
+        lo, hi = w_part(way, first)
+        copy(("w", way, first), w_hbm.at[lo:hi, :], w_rows(j, lo, hi), at(dx=way))
+
+    def w_take(way, first):
+        arrived(("w", way, first), w_rows(xj(-way), *w_part(way, first)))
+
+    for way in (1, -1):
+        w_send(way, True)
+    copy(("ws", 0), w_hbm, w_rows(j), at(flip=True))
+
+    res_load.wait()
+    res = res_ref[...]
+    fill = 128 - cols
+    if fill:
+        res = jnp.concatenate([res, jnp.zeros((fill, block), bf16)], axis=0)
+    ri = lax.broadcasted_iota(i32, (block, block), 0)
+    ci = lax.broadcasted_iota(i32, (block, block), 1)
+    eye = (ri == ci).astype(f32).astype(bf16)
+    rt_ref[...] = matmul(eye, res, NT).astype(bf16).reshape(GROUP, toks, 128)
+    for k in range(1, GROUP):
+        jj = (j + k) % GROUP
+        copy(("r", k), rt_ref.at[jj], rb_ref.at[j], (y, z * GROUP + jj))
+    for way in (1, -1):
+        w_send(way, False)
+
+    def z_first(name, part):
+        for d in (2, 1):
+            for way in (1, -1):
+                copy((name, -way * d), part(0, None), part(slot(-way * d), None), at(dz=way * d))
+
+    def z_second(name, part):
+        for way in (1, -1):
+            arrived((name, -2 * way), part(slot(-2 * way), None))
+            src = slot(-2 * way)
+            copy((name, -3 * way), part(src, None), part(slot(-3 * way), None), at(dz=way))
+            copy((name, 4, way), part(src, way), part(slot(4), way), at(dz=2 * way))
+
+    def z_near(name, part):
+        for way in (1, -1):
+            arrived((name, -way), part(slot(-way), None))
+
+    def z_far(name, part):
+        for way in (1, -1):
+            arrived((name, -3 * way), part(slot(-3 * way), None))
+            arrived((name, 4, way), part(slot(4), way))
+
+    feat = heads * vdim
+
+    def f_part(t):
+        def part(s, way):
+            c = slice(None) if way is None else slice(0, feat // 2) if way > 0 else slice(feat // 2, feat)
+            return feat_ref.at[s, t * branches : (t + 1) * branches, c]
+
+        return part
+
+    ro = lax.broadcasted_iota(i32, (rows, rows), 0)
+    co = lax.broadcasted_iota(i32, (rows, rows), 1)
+    swap = (co == (ro % branches) * heads + ro // branches).astype(f32).astype(bf16)
+    for t in range(trees):
         for c in tree_loads[t]:
             c.wait()
         q = q_ref[t]
@@ -249,7 +264,7 @@
         def soft(b, carry):
             r = pl.ds(pl.multiple_of(b * heads, heads), heads)
             st = s_ref[r, :trunk_len] * score_scale
-            sb = s_ref[r, trunk_len:] * score_scale + bias_ref[pl.ds(b, 1), :]
+            sb = s_ref[r, trunk_len:] * score_scale + bias_ref[t, pl.ds(b, 1), :]
             top = jnp.maximum(
                 jnp.max(st, axis=-1, keepdims=True), jnp.max(sb, axis=-1, keepdims=True)
             )
@@ -290,10 +305,15 @@
         chosen = (before[e : e + 1, :] == srow) & (marks[e : e + 1, :] > 0.5)
         onehot_ref[e * SLOTS : (e + 1) * SLOTS, :] = jnp.where(chosen, 1.0, 0.0).astype(bf16)
 
+    for way in (1, -1):
+        w_take(way, True)
+        w = w_rows(xj(-way), *w_part(way, True))
+        copy(("w2", way), w, w, at(dx=way))
     z_second("f0", f_part(0))
-    for d in (1, -1):
-        arrived(("w", d), w_rows(xj(-d)))
-        copy(("ws", d), w_rows(xj(-d)), w_rows(xj(-d)), at(flip=True))
+    for way in (1, -1):
+        w_take(way, False)
+        w = w_rows(xj(-way))
+        copy(("ws", way), w, w, at(flip=True))
     for t in range(1, trees):
         z_second("f%d" % t, f_part(t))
 
@@ -305,31 +325,38 @@
     )
     sum_ref[...] = residual
 
-    arrived(("w", 2), w_rows(xj(2)))
-    copy(("ws", 2), w_rows(xj(2)), w_rows(xj(2)), at(flip=True))
+    for way in (1, -1):
+        w = w_rows(xj(2), *w_part(way, True))
+        arrived(("w2", way), w)
+        copy(("ws2", way), w, w, at(flip=True))
     own_w.wait()
-    for d in (0, 1, -1, 2):
+    for d in (0, 1, -1):
         arrived(("ws", d), w_rows(xj_other(-d)))
+    for way in (1, -1):
+        arrived(("ws2", way), w_rows(xj_other(2), *w_part(way, True)))
     for t in range(trees):
         z_near("f%d" % t, f_part(t))
 
-    p_ids = [ids("p", d) for d in range(1, ny)]
-    assert p_ids[-1] - p_ids[0] == ny - 2
-
-    def part_copy(s, d):
+    ca = max(1, (cz * 5 // 7) // 128) * 128
+    parts_c = (slice(0, ca), slice(ca, cz))
+    p_ids = [ids("p", h, d) for h in range(2) for d in range(1, ny)]
+    assert p_ids[-1] - p_ids[0] == 2 * (ny - 1) - 1
+
+    def part_copy(s, h, d):
+        i = p_ids[0] + h * (ny - 1) + d - 1
         return pltpu.make_async_remote_copy(
-            src_ref=part16_ref.at[s],
-            dst_ref=got_ref.at[d - 1],
-            send_sem=send_sem.at[p_ids[0] + d - 1],
-            recv_sem=recv_sem.at[p_ids[0] + d - 1],
+            src_ref=part16_ref.at[s, :, parts_c[h]],
+            dst_ref=got_ref.at[d - 1, :, parts_c[h]],
+            send_sem=send_sem.at[i],
+            recv_sem=recv_sem.at[i],
             device_id=at(dy=d),
             device_id_type=MESH,
         )
 
-    def project(first, last):
+    def project(first, last, h):
         feats = feat_ref[first:last].reshape((last - first) * toks, feat)
-        for lo in range(0, cz, 256):
-            hi = min(cz, lo + 256)
+        for lo in range(parts_c[h].start, parts_c[h].stop, 256):
+            hi = min(parts_c[h].stop, lo + 256)
             prod = matmul(feats, w_ref[lo:hi, :], NT).reshape(last - first, toks, hi - lo)
             part_ref[first:last, :, lo:hi] = prod
             part16_ref[first:last, :, lo:hi] = prod.astype(bf16)
@@ -338,24 +365,27 @@
 
             @pl.when(d != 0)
             def _():
-                part_copy(s, d).start()
-
-    project(0, near)
-    for t in range(trees):
-        z_far("f%d" % t, f_part(t))
-    project(near, nz)
+                part_copy(s, h, d).start()
+
     dz_own = (y - z + nz) % nz
     own_slot = jnp.maximum(
         0, 2 * jnp.minimum(dz_own, nz - dz_own) - 1 + (dz_own > nz // 2).astype(i32)
     )
-    total = part_ref[own_slot]
-    for d in range(1, ny):
-        arrived(("p", d), got_ref.at[d - 1])
-        total = total + got_ref[d - 1].astype(f32)
-    hidden = (sum_ref[...] + total).astype(bf16)
-
-    ca = max(1, (cz * 5 // 7) // 128) * 128
-    h_ref[0, x, core] = hidden
+
+    def take_parts(h):
+        total = part_ref[own_slot, :, parts_c[h]]
+        for d in range(1, ny):
+            arrived(("p", h, d), got_ref.at[d - 1, :, parts_c[h]])
+            total = total + got_ref[d - 1, :, parts_c[h]].astype(f32)
+        h_ref[0, x, core, :, parts_c[h]] = (sum_ref[:, parts_c[h]] + total).astype(bf16)
+
+    project(0, near, 0)
+    for t in range(trees):
+        z_far("f%d" % t, f_part(t))
+    project(near, nz, 0)
+    project(0, near, 1)
+    project(near, nz, 1)
+    take_parts(0)
 
     def row_half(way):
         if way is None:
@@ -395,17 +425,18 @@
         arrived(("as", g), h_ref.at[c, :, 1 - core, :, :ca])
         arrived(("bs", g), h_ref.at[c, :, 1 - core, :, ca:])
 
+    z_first("a1", a1)
+    a2_send(0)
+    take_parts(1)
     for d in (2, 1, -1):
         copy(("b1", d), b1(0), b1(0), at(dx=d))
-    z_first("a1", a1)
-    a2_send(0)
+    z_second("a1", a1)
+    z_near("a1", a1)
+    a2_send(1)
     for d in (1, -1, 2):
         arrived(("b1", d), b1(-d))
     z_first("b2", b2)
     b_share(0)
-    z_second("a1", a1)
-    z_near("a1", a1)
-    a2_send(1)
     a2_take(0)
     z_second("b2", b2)
     z_near("b2", b2)
@@ -440,8 +471,9 @@
         at_z = pl.ds(pl.multiple_of(((z + REL[s] + nz) % nz) * cz, 128), cz)
         out_ref[:, at_z] = (picked_ref[s] * scale * gain_ref[:, at_z]).astype(bf16)
 
-    for d in range(1, ny):
-        part_copy(0, d).wait_send()
+    for h in range(2):
+        for d in range(1, ny):
+            part_copy(0, h, d).wait_send()
     for c in sends:
         c.wait_send()
     assert len(ids.names) <= sem_count
@@ -497,7 +529,7 @@
             pltpu.VMEM(expert_ids.shape[::-1], jnp.int32),
             pltpu.VMEM((rows, trunk_len + nkeys), f32),
             pltpu.VMEM((rows, trunk_len + nkeys), bf16),
-            pltpu.VMEM((branches, nkeys), f32),
+            pltpu.VMEM((trees, branches, nkeys), f32),
             pltpu.VMEM((heads, branches, lat), bf16),
             pltpu.VMEM((nz, toks, feat), bf16),
             pltpu.VMEM((cz, feat), bf16),

time: 83.2 us -> 75.4 us (0.906)
  Pallas kernels: 78.8 us -> 71 us
    pallas_call x1, Pallas kernels: 78.8 us -> 71 us  [shards(): pl.pallas_call(functools.partial(kernel, (ny, nz, sem_count)), out_shape=...]
where the time goes in v3:
time: 75.4 us; the launch traced here: 75.2 us
  Pallas kernels  71 us (94%)
  local copies, waits for them, and re-layouts  3.61 us (5%)
    pallas_call x1, Pallas kernels, shards(): pl.pallas_call(functools.partial(kernel, (ny, nz, sem_count)), out_shape=...  71 us
    unnamed x2, local copies, waits for them, and re-layouts  3.61 us

profile of v3, /device:TPU:1, one launch (start us, length us, event | category | flops | bytes accessed | tf_op | source)
XLA Modules:
  0.0 75.2 jit_solution(11428160406774076187)
XLA Ops:
  0.6 71.0 %decode_layer.1 = (bf16[112,256]{1,0:T(8,128)(2,1)}, bf16[64,7168]{1,0:T(8,128)(2,1)}) custom-call(bf16[2,256,576]{2,1,0:T(8,128)(2,1)} %bitcast.12, bf16[2,576,768]{2,1,0:T(8,128)(2,1)} %bitcast.9, bf16[2,512,576]{2,1,0:T(8,128)(2,1)} %bitcast.10, bf16[16,512,128]{2,1,0:T(8,128)(2,1)} %vup_hbm.1, bf16[112,2048]{1,0:T(8,128)(2,1)} %bitcast.13, ...), custom_call_target="tpu_custom_call" | custom-call | tf_op jit(solution)/shard_map/decode_layer/pallas_call | solution.py:512
  71.6 1.4 %copy.14 = bf16[256,112]{0,1:T(8,128)(2,1)} copy(bf16[256,112]{0,1:T(8,128)(2,1)} %bitcast.15) | data formatting | bytes 114688
  73.1 2.2 %copy.15 = bf16[1,4,16,7168]{3,2,1,0:T(8,128)(2,1)} copy(bf16[1,4,16,7168]{3,2,1,0:T(8,128)(2,1)} %bitcast.11) | data formatting | bytes 1835008

commit v4 on v3

--- a/solution.py
+++ b/solution.py
@@ -122,8 +122,16 @@
         loads.append(c)
         return c
 
-    def w_rows(jj, lo=0, hi=cols):
-        return w_ref.at[pl.ds(pl.multiple_of(jj * cols + lo, 16), hi - lo), :]
+    ORDER = (0, 1, -1, 2)
+
+    def xj(dx):
+        return ORDER.index(dx) * 2 + core
+
+    def xj_other(dx):
+        return ORDER.index(dx) * 2 + 1 - core
+
+    def w_rows(jj, k=slice(None)):
+        return w_ref.at[pl.ds(pl.multiple_of(jj * cols, 16), cols), k]
 
     res_load = load(res_hbm, res_ref)
     mask_loads = [load(vis_hbm, vis_ref), load(len_hbm, len_ref)]
@@ -137,7 +145,7 @@
             ]
         )
     vup_load = load(vup_hbm, vup_ref)
-    own_w = load(w_hbm, w_rows(j))
+    own_w = load(w_hbm, w_rows(xj(0)))
     late_loads = [load(ids_hbm, ids_ref), load(gain_hbm, gain_ref)]
 
     sends = []
@@ -182,79 +190,7 @@
         live = (vis > 0) & (pos < lim)
         bias_ref[t] = jnp.where(live, 0.0, -1e30)
 
-    pl.semaphore_wait(barrier, len(partners))
-
-    def xj(dx):
-        return ((x + dx + NX) % NX) * 2 + core
-
-    def xj_other(dx):
-        return ((x + dx + NX) % NX) * 2 + (1 - core)
-
-    w_cut = (cols // 16 + 1) // 2 * 16
-
-    def w_part(way, first):
-        return (0, w_cut) if (way > 0) == first else (w_cut, cols)
-
-    def w_send(way, first):
-        lo, hi = w_part(way, first)
-        copy(("w", way, first), w_hbm.at[lo:hi, :], w_rows(j, lo, hi), at(dx=way))
-
-    def w_take(way, first):
-        arrived(("w", way, first), w_rows(xj(-way), *w_part(way, first)))
-
-    for way in (1, -1):
-        w_send(way, True)
-    copy(("ws", 0), w_hbm, w_rows(j), at(flip=True))
-
-    res_load.wait()
-    res = res_ref[...]
-    fill = 128 - cols
-    if fill:
-        res = jnp.concatenate([res, jnp.zeros((fill, block), bf16)], axis=0)
-    ri = lax.broadcasted_iota(i32, (block, block), 0)
-    ci = lax.broadcasted_iota(i32, (block, block), 1)
-    eye = (ri == ci).astype(f32).astype(bf16)
-    rt_ref[...] = matmul(eye, res, NT).astype(bf16).reshape(GROUP, toks, 128)
-    for k in range(1, GROUP):
-        jj = (j + k) % GROUP
-        copy(("r", k), rt_ref.at[jj], rb_ref.at[j], (y, z * GROUP + jj))
-    for way in (1, -1):
-        w_send(way, False)
-
-    def z_first(name, part):
-        for d in (2, 1):
-            for way in (1, -1):
-                copy((name, -way * d), part(0, None), part(slot(-way * d), None), at(dz=way * d))
-
-    def z_second(name, part):
-        for way in (1, -1):
-            arrived((name, -2 * way), part(slot(-2 * way), None))
-            src = slot(-2 * way)
-            copy((name, -3 * way), part(src, None), part(slot(-3 * way), None), at(dz=way))
-            copy((name, 4, way), part(src, way), part(slot(4), way), at(dz=2 * way))
-
-    def z_near(name, part):
-        for way in (1, -1):
-            arrived((name, -way), part(slot(-way), None))
-
-    def z_far(name, part):
-        for way in (1, -1):
-            arrived((name, -3 * way), part(slot(-3 * way), None))
-            arrived((name, 4, way), part(slot(4), way))
-
-    feat = heads * vdim
-
-    def f_part(t):
-        def part(s, way):
-            c = slice(None) if way is None else slice(0, feat // 2) if way > 0 else slice(feat // 2, feat)
-            return feat_ref.at[s, t * branches : (t + 1) * branches, c]
-
-        return part
-
-    ro = lax.broadcasted_iota(i32, (rows, rows), 0)
-    co = lax.broadcasted_iota(i32, (rows, rows), 1)
-    swap = (co == (ro % branches) * heads + ro // branches).astype(f32).astype(bf16)
-    for t in range(trees):
+    def scores(t):
         for c in tree_loads[t]:
             c.wait()
         q = q_ref[t]
@@ -278,6 +214,75 @@
             return carry
 
         lax.fori_loop(0, branches, soft, 0, unroll=4)
+
+    scores(0)
+    pl.semaphore_wait(barrier, len(partners))
+
+    k_half = heads * vdim // 2
+
+    def w_part(way, first):
+        return slice(0, k_half) if (way > 0) == first else slice(k_half, 2 * k_half)
+
+    def w_send(way, first):
+        k = w_part(way, first)
+        copy(("w", way, first), w_hbm.at[:, k], w_rows(xj(-way), k), at(dx=way))
+
+    def w_take(way, first):
+        arrived(("w", way, first), w_rows(xj(-way), w_part(way, first)))
+
+    for way in (1, -1):
+        w_send(way, True)
+    copy(("ws", 0), w_hbm, w_rows(xj(0)), at(flip=True))
+
+    res_load.wait()
+    res = res_ref[...]
+    fill = 128 - cols
+    if fill:
+        res = jnp.concatenate([res, jnp.zeros((fill, block), bf16)], axis=0)
+    ri = lax.broadcasted_iota(i32, (block, block), 0)
+    ci = lax.broadcasted_iota(i32, (block, block), 1)
+    eye = (ri == ci).astype(f32).astype(bf16)
+    rt_ref[...] = matmul(eye, res, NT).astype(bf16).reshape(GROUP, toks, 128)
+    for k in range(1, GROUP):
+        jj = (j + k) % GROUP
+        copy(("r", k), rt_ref.at[jj], rb_ref.at[j], (y, z * GROUP + jj))
+
+    def z_first(name, part):
+        for d in (2, 1):
+            for way in (1, -1):
+                copy((name, -way * d), part(0, None), part(slot(-way * d), None), at(dz=way * d))
+
+    def z_second(name, part):
+        for way in (1, -1):
+            arrived((name, -2 * way), part(slot(-2 * way), None))
+            src = slot(-2 * way)
+            copy((name, -3 * way), part(src, None), part(slot(-3 * way), None), at(dz=way))
+            copy((name, 4, way), part(src, way), part(slot(4), way), at(dz=2 * way))
+
+    def z_near(name, part):
+        for way in (1, -1):
+            arrived((name, -way), part(slot(-way), None))
+
+    def z_far(name, part):
+        for way in (1, -1):
+            arrived((name, -3 * way), part(slot(-3 * way), None))
+            arrived((name, 4, way), part(slot(4), way))
+
+    feat = heads * vdim
+
+    def f_part(t):
+        def part(s, way):
+            c = slice(None) if way is None else slice(0, feat // 2) if way > 0 else slice(feat // 2, feat)
+            return feat_ref.at[s, t * branches : (t + 1) * branches, c]
+
+        return part
+
+    ro = lax.broadcasted_iota(i32, (rows, rows), 0)
+    co = lax.broadcasted_iota(i32, (rows, rows), 1)
+    swap = (co == (ro % branches) * heads + ro // branches).astype(f32).astype(bf16)
+    for t in range(trees):
+        if t > 0:
+            scores(t)
         o = matmul(p_ref[:, :trunk_len], trunk_ref[t, :lat, :], NT)
         o = o + matmul(p_ref[:, trunk_len:], branch_ref[t, :, :lat])
         o = matmul(swap, o.astype(bf16)).astype(bf16)
@@ -288,6 +293,9 @@
             f = matmul(lat_ref[h], vup_ref[h])
             feat_ref[0, t * branches : (t + 1) * branches, h * vdim : (h + 1) * vdim] = f.astype(bf16)
         z_first("f%d" % t, f_part(t))
+        if t == 0:
+            for way in (1, -1):
+                w_send(way, False)
 
     for c in late_loads:
         c.wait()
@@ -307,8 +315,8 @@
 
     for way in (1, -1):
         w_take(way, True)
-        w = w_rows(xj(-way), *w_part(way, True))
-        copy(("w2", way), w, w, at(dx=way))
+        k = w_part(way, True)
+        copy(("w2", way), w_rows(xj(-way), k), w_rows(xj(2), k), at(dx=way))
     z_second("f0", f_part(0))
     for way in (1, -1):
         w_take(way, False)
@@ -321,159 +329,203 @@
     for k in range(1, GROUP):
         arrived(("r", k), rb_ref.at[(j + GROUP - k) % GROUP])
     residual = jnp.concatenate(
-        [rb_ref[g].astype(f32)[:, :cols] for g in range(GROUP)], axis=1
+        [
+            rb_ref[((x + d + NX) % NX) * 2 + c].astype(f32)[:, :cols]
+            for d in ORDER
+            for c in range(2)
+        ],
+        axis=1,
     )
     sum_ref[...] = residual
 
-    for way in (1, -1):
-        w = w_rows(xj(2), *w_part(way, True))
-        arrived(("w2", way), w)
-        copy(("ws2", way), w, w, at(flip=True))
     own_w.wait()
     for d in (0, 1, -1):
         arrived(("ws", d), w_rows(xj_other(-d)))
-    for way in (1, -1):
-        arrived(("ws2", way), w_rows(xj_other(2), *w_part(way, True)))
-    for t in range(trees):
-        z_near("f%d" % t, f_part(t))
-
-    ca = max(1, (cz * 5 // 7) // 128) * 128
-    parts_c = (slice(0, ca), slice(ca, cz))
-    p_ids = [ids("p", h, d) for h in range(2) for d in range(1, ny)]
-    assert p_ids[-1] - p_ids[0] == 2 * (ny - 1) - 1
-
-    def part_copy(s, h, d):
-        i = p_ids[0] + h * (ny - 1) + d - 1
+
+    def tree_rows(t):
+        return slice(t * branches, (t + 1) * branches)
+
+    cut = cz * 3 // 4 // 128 * 128
+    halves = (slice(0, cut), slice(cut, cz))
+    p_ids = [ids("p", t, h, d) for t in range(trees) for h in range(2) for d in range(1, ny)]
+    assert p_ids[-1] - p_ids[0] == 2 * trees * (ny - 1) - 1
+
+    def part_copy(s, t, h, d):
+        i = p_ids[0] + (2 * t + h) * (ny - 1) + d - 1
         return pltpu.make_async_remote_copy(
-            src_ref=part16_ref.at[s, :, parts_c[h]],
-            dst_ref=got_ref.at[d - 1, :, parts_c[h]],
+            src_ref=part16_ref.at[s, tree_rows(t), halves[h]],
+            dst_ref=got_ref.at[d - 1, tree_rows(t), halves[h]],
             send_sem=send_sem.at[i],
             recv_sem=recv_sem.at[i],
             device_id=at(dy=d),
             device_id_type=MESH,
         )
 
-    def project(first, last, h):
-        feats = feat_ref[first:last].reshape((last - first) * toks, feat)
-        for lo in range(parts_c[h].start, parts_c[h].stop, 256):
-            hi = min(parts_c[h].stop, lo + 256)
-            prod = matmul(feats, w_ref[lo:hi, :], NT).reshape(last - first, toks, hi - lo)
-            part_ref[first:last, :, lo:hi] = prod
-            part16_ref[first:last, :, lo:hi] = prod.astype(bf16)
+    def project(first, last, t, h):
+        feats = feat_ref[first:last, tree_rows(t), :].reshape((last - first) * branches, feat)
+        for lo in range(halves[h].start, halves[h].stop, 256):
+            hi = min(halves[h].stop, lo + 256)
+            prod = matmul(feats, w_ref[lo:hi, :], NT).reshape(last - first, branches, hi - lo)
+            part_ref[first:last, tree_rows(t), lo:hi] = prod
+            part16_ref[first:last, tree_rows(t), lo:hi] = prod.astype(bf16)
         for s in range(first, last):
             d = (z + REL[s] - y + 2 * ny) % ny
 
             @pl.when(d != 0)
             def _():
-                part_copy(s, h, d).start()
+                part_copy(s, t, h, d).start()
 
     dz_own = (y - z + nz) % nz
     own_slot = jnp.maximum(
         0, 2 * jnp.minimum(dz_own, nz - dz_own) - 1 + (dz_own > nz // 2).astype(i32)
     )
 
-    def take_parts(h):
-        total = part_ref[own_slot, :, parts_c[h]]
+    def take_parts(t):
+        r = tree_rows(t)
+        total = part_ref[own_slot, r, :]
         for d in range(1, ny):
-            arrived(("p", h, d), got_ref.at[d - 1, :, parts_c[h]])
-            total = total + got_ref[d - 1, :, parts_c[h]].astype(f32)
-        h_ref[0, x, core, :, parts_c[h]] = (sum_ref[:, parts_c[h]] + total).astype(bf16)
-
-    project(0, near, 0)
+            for h in range(2):
+                arrived(("p", t, h, d), got_ref.at[d - 1, r, halves[h]])
+            total = total + got_ref[d - 1, r, :].astype(f32)
+        total = sum_ref[r, :] + total
+        pair = 2 * cols
+        hidden = total
+        for at_x in range(NX):
+            places = [ORDER.index((k - at_x + 1) % NX - 1) for k in range(NX)]
+            turned = jnp.concatenate([total[:, p * pair : (p + 1) * pair] for p in places], axis=1)
+            hidden = jnp.where(x == at_x, turned, hidden)
+        h_ref[0, x, core, r, :] = hidden.astype(bf16)
+
+    for t in range(trees):
+        z_near("f%d" % t, f_part(t))
+        project(0, near, t, 0)
     for t in range(trees):
         z_far("f%d" % t, f_part(t))
-    project(near, nz, 0)
-    project(0, near, 1)
-    project(near, nz, 1)
+        project(near, nz, t, 0)
+    for way in (1, -1):
+        w = w_rows(xj(2), w_part(way, True))
+        arrived(("w2", way), w)
+        copy(("ws2", way), w, w, at(flip=True))
+    for way in (1, -1):
+        arrived(("ws2", way), w_rows(xj_other(2), w_part(way, True)))
+    for t in range(trees):
+        project(0, nz, t, 1)
     take_parts(0)
 
-    def row_half(way):
-        if way is None:
-            return slice(None)
-        return slice(0, toks // 2) if way > 0 else slice(toks // 2, toks)
-
-    def a1(s, way):
-        return h_ref.at[s, x, core, row_half(way), :ca]
-
-    def b2(s, way):
-        return h_ref.at[s, :, core, row_half(way), ca:]
-
-    def b1(dx):
-        return h_ref.at[0, (x + dx + NX) % NX, core, :, ca:]
-
-    parts_z = ((0, 1), (1, near), (near, nz))
-
-    def a2(g, dx):
-        return h_ref.at[parts_z[g][0] : parts_z[g][1], (x + dx + NX) % NX, core, :, :ca]
-
-    def a2_send(g):
-        for d in (2, 1, -1):
-            copy(("a2", g, d), a2(g, 0), a2(g, 0), at(dx=d))
-
-    def a2_take(g):
-        for d in (1, -1, 2):
-            arrived(("a2", g, d), a2(g, -d))
-        s = h_ref.at[parts_z[g][0] : parts_z[g][1], :, core, :, :ca]
-        copy(("as", g), s, s, at(flip=True))
-
-    def b_share(g):
-        s = h_ref.at[parts_z[g][0] : parts_z[g][1], :, core, :, ca:]
-        copy(("bs", g), s, s, at(flip=True))
-
-    def shared(g):
-        c = slice(parts_z[g][0], parts_z[g][1])
-        arrived(("as", g), h_ref.at[c, :, 1 - core, :, :ca])
-        arrived(("bs", g), h_ref.at[c, :, 1 - core, :, ca:])
-
-    z_first("a1", a1)
-    a2_send(0)
+    assert trees == 2
+    ca = (cz * 3 // 7) // 128 * 128
+    whole = slice(0, cz)
+    low, high = slice(0, ca), slice(ca, cz)
+    three = ((0, 1), (1, near), (near, nz))
+    two = ((0, near), (near, nz))
+
+    def half_cols(c, way):
+        cut = c.start + ((c.stop - c.start) // 128 + 1) // 2 * 128
+        return c if way is None else slice(c.start, cut) if way > 0 else slice(cut, c.stop)
+
+    def x_at(dx):
+        return (x + dx + NX) % NX
+
+    class Region:
+        def __init__(self, name, t, c, groups):
+            self.name, self.r, self.c, self.groups = name, tree_rows(t), c, groups
+
+        def own(self, s, way):
+            return h_ref.at[s, x, core, self.r, half_cols(self.c, way)]
+
+        def every_x(self, s, way):
+            return h_ref.at[s, :, core, self.r, half_cols(self.c, way)]
+
+        def one_x(self, g, dx):
+            lo, hi = self.groups[g]
+            return h_ref.at[lo:hi, x_at(dx), core, self.r, self.c]
+
+        def all_x(self, g, cc):
+            lo, hi = self.groups[g]
+            return h_ref.at[lo:hi, :, cc, self.r, self.c]
+
+        def x_send(self, g):
+            for d in (2, 1, -1):
+                copy((self.name, "x", g, d), self.one_x(g, 0), self.one_x(g, 0), at(dx=d))
+
+        def x_take(self, g):
+            for d in (1, -1, 2):
+                arrived((self.name, "x", g, d), self.one_x(g, -d))
+
+        def share(self, g):
+            copy((self.name, "s", g), self.all_x(g, core), self.all_x(g, core), at(flip=True))
+
+        def shared(self, g):
+            arrived((self.name, "s", g), self.all_x(g, 1 - core))
+
+    ra = Region("a", 0, whole, three)
+    rc = Region("c", 1, low, two)
+    rb = Region("b", 1, high, three)
+    z_first("az", ra.own)
+    ra.x_send(0)
     take_parts(1)
-    for d in (2, 1, -1):
-        copy(("b1", d), b1(0), b1(0), at(dx=d))
-    z_second("a1", a1)
-    z_near("a1", a1)
-    a2_send(1)
-    for d in (1, -1, 2):
-        arrived(("b1", d), b1(-d))
-    z_first("b2", b2)
-    b_share(0)
-    a2_take(0)
-    z_second("b2", b2)
-    z_near("b2", b2)
-    b_share(1)
-    z_far("a1", a1)
-    a2_send(2)
-    a2_take(1)
-    shared(0)
+    rb.x_send(0)
+    z_first("cz", rc.own)
+    z_second("az", ra.own)
+    z_near("az", ra.own)
+    ra.x_send(1)
+    rb.x_take(0)
+    z_first("bz", rb.every_x)
+    rb.share(0)
+    z_second("cz", rc.own)
+    z_near("cz", rc.own)
+    rc.x_send(0)
+    z_far("az", ra.own)
+    ra.x_send(2)
+    ra.x_take(0)
+    ra.share(0)
+    ra.x_take(1)
+    ra.share(1)
+    z_second("bz", rb.every_x)
+    z_near("bz", rb.every_x)
+    rb.share(1)
+    z_far("cz", rc.own)
+    rc.x_send(1)
+    rc.x_take(0)
+    rc.share(0)
+    ra.x_take(2)
+    ra.share(2)
+
+    def pick(first, last, squares):
+        for s in range(first, last):
+            got = matmul(onehot_ref[...], h_ref[s].reshape(block, cz))
+            picked_ref[s] = got
+            squares = squares + jnp.sum(got * got, axis=-1, keepdims=True)
+        return squares
+
+    for g in range(2):
+        ra.shared(g)
+        rb.shared(g)
+    rc.shared(0)
+    squares = pick(0, near, jnp.zeros((EXP_DEV * SLOTS, 1), f32))
 
     si = lax.broadcasted_iota(i32, (cols, cz), 0)
     sc = lax.broadcasted_iota(i32, (cols, cz), 1)
     mine = (sc == si + j * cols).astype(f32).astype(bf16)
     hid_ref[...] = matmul(mine, h_ref[0].reshape(block, cz), NT).astype(bf16)
 
-    def pick(g, squares):
-        for s in range(*parts_z[g]):
-            got = matmul(onehot_ref[...], h_ref[s].reshape(block, cz))
-            picked_ref[s] = got
-            squares = squares + jnp.sum(got * got, axis=-1, keepdims=True)
-        return squares
-
-    squares = pick(0, jnp.zeros((EXP_DEV * SLOTS, 1), f32))
-    z_far("b2", b2)
-    b_share(2)
-    shared(1)
-    squares = pick(1, squares)
-    a2_take(2)
-    shared(2)
-    squares = pick(2, squares)
+    rc.x_take(1)
+    rc.share(1)
+    z_far("bz", rb.every_x)
+    rb.share(2)
+    ra.shared(2)
+    rc.shared(1)
+    rb.shared(2)
+    squares = pick(near, nz, squares)
     scale = lax.rsqrt(squares / width + norm_eps)
     for s in range(nz):
         at_z = pl.ds(pl.multiple_of(((z + REL[s] + nz) % nz) * cz, 128), cz)
         out_ref[:, at_z] = (picked_ref[s] * scale * gain_ref[:, at_z]).astype(bf16)
 
-    for h in range(2):
-        for d in range(1, ny):
-            part_copy(0, h, d).wait_send()
+    for t in range(trees):
+        for h in range(2):
+            for d in range(1, ny):
+                part_copy(0, t, h, d).wait_send()
     for c in sends:
         c.wait_send()
     assert len(ids.names) <= sem_count
@@ -505,7 +557,7 @@
     cz = GROUP * cols
     width = nz * cz
     bf16, f32 = jnp.bfloat16, jnp.float32
-    sem_count = 96
+    sem_count = 160
     hbm = pl.BlockSpec(memory_space=pl.ANY)
     vmem = pl.BlockSpec(memory_space=pltpu.VMEM)
     chosen = EXP_DEV * SLOTS

time: 75.4 us -> 75.3 us (level)
  no operation moved by 1% of the time
where the time goes in v4:
time: 75.3 us; the launch traced here: 75.1 us
  Pallas kernels  70.9 us (94%)
  local copies, waits for them, and re-layouts  3.61 us (5%)
    pallas_call x1, Pallas kernels, shards(): pl.pallas_call(functools.partial(kernel, (ny, nz, sem_count)), out_shape=...  70.9 us
    unnamed x2, local copies, waits for them, and re-layouts  3.61 us

profile of v4, /device:TPU:1, one launch (start us, length us, event | category | flops | bytes accessed | tf_op | source)
XLA Modules:
  0.0 75.1 jit_solution(4738800059559341532)
XLA Ops:
  0.6 70.9 %decode_layer.1 = (bf16[112,256]{1,0:T(8,128)(2,1)}, bf16[64,7168]{1,0:T(8,128)(2,1)}) custom-call(bf16[2,256,576]{2,1,0:T(8,128)(2,1)} %bitcast.12, bf16[2,576,768]{2,1,0:T(8,128)(2,1)} %bitcast.9, bf16[2,512,576]{2,1,0:T(8,128)(2,1)} %bitcast.10, bf16[16,512,128]{2,1,0:T(8,128)(2,1)} %vup_hbm.1, bf16[112,2048]{1,0:T(8,128)(2,1)} %bitcast.13, ...), custom_call_target="tpu_custom_call" | custom-call | tf_op jit(solution)/shard_map/decode_layer/pallas_call | solution.py:564
  71.5 1.4 %copy.14 = bf16[256,112]{0,1:T(8,128)(2,1)} copy(bf16[256,112]{0,1:T(8,128)(2,1)} %bitcast.15) | data formatting | bytes 114688
  73.0 2.2 %copy.15 = bf16[1,4,16,7168]{3,2,1,0:T(8,128)(2,1)} copy(bf16[1,4,16,7168]{3,2,1,0:T(8,128)(2,1)} %bitcast.11) | data formatting | bytes 1835008

commit v5 on v4

--- a/solution.py
+++ b/solution.py
@@ -413,7 +413,7 @@
     take_parts(0)
 
     assert trees == 2
-    ca = (cz * 3 // 7) // 128 * 128
+    ca = (cz * 2 // 7) // 128 * 128
     whole = slice(0, cz)
     low, high = slice(0, ca), slice(ca, cz)
     three = ((0, 1), (1, near), (near, nz))
@@ -529,6 +529,24 @@
     for c in sends:
         c.wait_send()
     assert len(ids.names) <= sem_count
+
+
+def hand_over(hid_in, rows_in, hid_out, rows_out, hid_ref, rows_ref, in_sem, out_sem):
+    pieces = rows_in.shape[0] // SLOTS
+    moves = []
+    for i in range(pieces):
+        r = slice(i * SLOTS, (i + 1) * SLOTS)
+        moves.append((rows_in.at[r], rows_ref.at[r], rows_out.at[r]))
+    moves.append((hid_in, hid_ref, hid_out))
+    ins = [pltpu.make_async_copy(m[0], m[1], in_sem.at[i]) for i, m in enumerate(moves)]
+    outs = [pltpu.make_async_copy(m[1], m[2], out_sem.at[i]) for i, m in enumerate(moves)]
+    for c in ins:
+        c.start()
+    for c, o in zip(ins, outs):
+        c.wait()
+        o.start()
+    for o in outs:
+        o.wait()
 
 
 def shards(
@@ -614,6 +632,23 @@
         norm_gain.reshape(1, width),
         expert_ids.T,
     )
+    hidden, rows_out = pl.pallas_call(
+        hand_over,
+        out_shape=(
+            jax.ShapeDtypeStruct(hidden.shape, bf16),
+            jax.ShapeDtypeStruct(rows_out.shape, bf16),
+        ),
+        in_specs=[hbm] * 2,
+        out_specs=(hbm, hbm),
+        scratch_shapes=[
+            pltpu.VMEM(hidden.shape, bf16),
+            pltpu.VMEM(rows_out.shape, bf16),
+            pltpu.SemaphoreType.DMA((EXP_DEV + 1,)),
+            pltpu.SemaphoreType.DMA((EXP_DEV + 1,)),
+        ],
+        compiler_params=pltpu.CompilerParams(vmem_limit_bytes=63 * 1024 * 1024),
+        name="hand_over",
+    )(hidden, rows_out)
     return hidden.T, rows_out.reshape(1, EXP_DEV, SLOTS, width)
 
 

time: 75.3 us -> 72.4 us (0.961)
  local copies, waits for them, and re-layouts: 3.61 us -> 0 us
    unnamed x2 -> x0, local copies, waits for them, and re-layouts: 3.61 us -> none
    pallas_call x0 -> x1, Pallas kernels: none -> 2.06 us  [shards(): pl.pallas_call(hand_over, out_shape=(jax.ShapeDtypeStruct(hidden.shape, b...]
    pallas_call x1, Pallas kernels: 70.9 us -> 69.5 us  [shards(): pl.pallas_call(functools.partial(kernel, (ny, nz, sem_count)), out_shape=...]
where the time goes in v5:
time: 72.4 us; the launch traced here: 72.2 us
  Pallas kernels  71.6 us (99%)
    pallas_call x1, Pallas kernels, shards(): pl.pallas_call(functools.partial(kernel, (ny, nz, sem_count)), out_shape=...  69.5 us
    pallas_call x1, Pallas kernels, shards(): pl.pallas_call(hand_over, out_shape=(jax.ShapeDtypeStruct(hidden.shape, b...  2.06 us

profile of v5, /device:TPU:1, one launch (start us, length us, event | category | flops | bytes accessed | tf_op | source)
XLA Modules:
  0.0 72.2 jit_solution(3963275017648119508)
XLA Ops:
  0.6 69.5 %decode_layer.1 = (bf16[112,256]{1,0:T(8,128)(2,1)}, bf16[64,7168]{1,0:T(8,128)(2,1)}) custom-call(bf16[2,256,576]{2,1,0:T(8,128)(2,1)} %bitcast.11, bf16[2,576,768]{2,1,0:T(8,128)(2,1)} %bitcast.9, bf16[2,512,576]{2,1,0:T(8,128)(2,1)} %bitcast.10, bf16[16,512,128]{2,1,0:T(8,128)(2,1)} %vup_hbm.1, bf16[112,2048]{1,0:T(8,128)(2,1)} %bitcast.12, ...), custom_call_target="tpu_custom_call" | custom-call | tf_op jit(solution)/shard_map/decode_layer/pallas_call | solution.py:582
  70.2 2.1 %hand_over.1 = (bf16[112,256]{1,0:T(8,128)(2,1)}, bf16[64,7168]{1,0:T(8,128)(2,1)}) custom-call(bf16[112,256]{1,0:T(8,128)(2,1)} %get-tuple-element.6.hid_in, bf16[64,7168]{1,0:T(8,128)(2,1)} %get-tuple-element.7.rows_in), custom_call_target="tpu_custom_call" | custom-call | tf_op jit(solution)/shard_map/hand_over/pallas_call | solution.py:635

commit v6 on v5

--- a/solution.py
+++ b/solution.py
@@ -44,8 +44,8 @@
     res_hbm,
     gain_hbm,
     ids_hbm,
-    hid_ref,
-    out_ref,
+    hid_hbm,
+    out_hbm,
     q_ref,
     trunk_ref,
     branch_ref,
@@ -70,6 +70,9 @@
     h_ref,
     onehot_ref,
     picked_ref,
+    hid_ref,
+    out_ref,
+    out_sem,
     in_sem,
     send_sem,
     recv_sem,
@@ -508,6 +511,8 @@
     sc = lax.broadcasted_iota(i32, (cols, cz), 1)
     mine = (sc == si + j * cols).astype(f32).astype(bf16)
     hid_ref[...] = matmul(mine, h_ref[0].reshape(block, cz), NT).astype(bf16)
+    results = [pltpu.make_async_copy(hid_ref, hid_hbm, out_sem.at[nz])]
+    results[0].start()
 
     rc.x_take(1)
     rc.share(1)
@@ -520,12 +525,16 @@
     scale = lax.rsqrt(squares / width + norm_eps)
     for s in range(nz):
         at_z = pl.ds(pl.multiple_of(((z + REL[s] + nz) % nz) * cz, 128), cz)
-        out_ref[:, at_z] = (picked_ref[s] * scale * gain_ref[:, at_z]).astype(bf16)
+        out_ref[s] = (picked_ref[s] * scale * gain_ref[:, at_z]).astype(bf16)
+        results.append(pltpu.make_async_copy(out_ref.at[s], out_hbm.at[:, at_z], out_sem.at[s]))
+        results[-1].start()
 
     for t in range(trees):
         for h in range(2):
             for d in range(1, ny):
                 part_copy(0, t, h, d).wait_send()
+    for c in results:
+        c.wait()
     for c in sends:
         c.wait_send()
     assert len(ids.names) <= sem_count
@@ -577,7 +586,6 @@
     bf16, f32 = jnp.bfloat16, jnp.float32
     sem_count = 160
     hbm = pl.BlockSpec(memory_space=pl.ANY)
-    vmem = pl.BlockSpec(memory_space=pltpu.VMEM)
     chosen = EXP_DEV * SLOTS
     hidden, rows_out = pl.pallas_call(
         functools.partial(kernel, (ny, nz, sem_count)),
@@ -586,7 +594,7 @@
             jax.ShapeDtypeStruct((chosen, width), bf16),
         ),
         in_specs=[hbm] * 10,
-        out_specs=(vmem, vmem),
+        out_specs=(hbm, hbm),
         scratch_shapes=[
             pltpu.VMEM((trees, rows, kdim), bf16),
             pltpu.VMEM((trees, kdim, trunk_len), bf16),
@@ -612,6 +620,9 @@
             pltpu.VMEM((nz, NX, 2, toks, cz), bf16),
             pltpu.VMEM((chosen, block), bf16),
             pltpu.VMEM((nz, chosen, cz), f32),
+            pltpu.VMEM((cols, block), bf16),
+            pltpu.VMEM((nz, chosen, cz), bf16),
+            pltpu.SemaphoreType.DMA((nz + 1,)),
             pltpu.SemaphoreType.DMA((16,)),
             pltpu.SemaphoreType.DMA((sem_count,)),
             pltpu.SemaphoreType.DMA((sem_count,)),

time: 72.4 us -> 72.2 us (level)
  no operation moved by 1% of the time
where the time goes in v6:
time: 72.2 us; the launch traced here: 72.1 us
  Pallas kernels  71.5 us (99%)
    pallas_call x1, Pallas kernels, shards(): pl.pallas_call(functools.partial(kernel, (ny, nz, sem_count)), out_shape=...  69.4 us
    pallas_call x1, Pallas kernels, shards(): pl.pallas_call(hand_over, out_shape=(jax.ShapeDtypeStruct(hidden.shape, b...  2.06 us

profile of v6, /device:TPU:1, one launch (start us, length us, event | category | flops | bytes accessed | tf_op | source)
XLA Modules:
  0.0 72.1 jit_solution(7881145428643097399)
XLA Ops:
  0.6 69.4 %decode_layer.1 = (bf16[112,256]{1,0:T(8,128)(2,1)}, bf16[64,7168]{1,0:T(8,128)(2,1)}) custom-call(bf16[2,256,576]{2,1,0:T(8,128)(2,1)} %bitcast.11, bf16[2,576,768]{2,1,0:T(8,128)(2,1)} %bitcast.9, bf16[2,512,576]{2,1,0:T(8,128)(2,1)} %bitcast.10, bf16[16,512,128]{2,1,0:T(8,128)(2,1)} %vup_hbm.1, bf16[112,2048]{1,0:T(8,128)(2,1)} %bitcast.12, ...), custom_call_target="tpu_custom_call" | custom-call | tf_op jit(solution)/shard_map/decode_layer/pallas_call | solution.py:590
  70.0 2.1 %hand_over.1 = (bf16[112,256]{1,0:T(8,128)(2,1)}, bf16[64,7168]{1,0:T(8,128)(2,1)}) custom-call(bf16[112,256]{1,0:T(8,128)(2,1)} %get-tuple-element.6.hid_in, bf16[64,7168]{1,0:T(8,128)(2,1)} %get-tuple-element.7.rows_in), custom_call_target="tpu_custom_call" | custom-call | tf_op jit(solution)/shard_map/hand_over/pallas_call | solution.py:646
